TPU v7x, 256 devices: a whole 4x4x8 slice. The times are simulated.
256 devices in a mesh: seq: 16 (over y, x), exp: 16 (over z, core).
Axes of the slice: x: 4, y: 4, z: 8, core: 2. Of those that a mesh axis runs over, the one named last changes fastest.
Arguments:
- queries: bfloat16 [2048, 4096], P('seq', 'exp'), may hold values from -4 to 4
- keyvals: bfloat16 [2048, 2, 512], P('seq'), may hold values from -2.5 to 2.5
- sinks: float32 [64], P('exp'), may hold values from -3 to 3
- out_proj: bfloat16 [4096, 2880], P('exp'), may hold values from -0.75 to 0.75
- residual: bfloat16 [2048, 2880], P('seq', 'exp'), may hold values from -20 to 20
- norm_gain: float32 [2880], P('exp'), may hold values from 0.1 to 1.9
- router_weight: float32 [2880, 32], P('exp'), may hold values from -0.109375 to 0.109375
- route_ids: int32 [2048, 4], P('seq'), may hold values from 0 to 31, all different within a row; in each aligned block of 128 rows (0 to 127, 128 to 255, ...) at most 32 rows name the same one
- expert_in: bfloat16 [256, 2880, 2, 360], P(('seq', 'exp')), may hold values from -0.109375 to 0.109375
- expert_out: bfloat16 [256, 360, 2880], P(('seq', 'exp')), may hold values from -0.109375 to 0.109375
Outputs:
- mixed: bfloat16 [2048, 2880], P('seq', 'exp')
Inputs may be any that keep to these rules, and one draw needn't show every extreme that they name: `route_ids`: each row names 4 different experts; within each aligned block of 128 rows no expert is named by more than 32 rows, a bound that some block reaches.
All inputs are finite; a program needn't handle non-finite values.
Results may differ from a plain program's by a relative error of at most 0.015.
Values may be sent and summed in bfloat16 or wider, within the bound.
A program may use at most 128 MiB of HBM per device.

v0:
```python
import jax
import jax.numpy as jnp
from jax import lax
from jax.sharding import PartitionSpec as P

D = 2880
HEADS = 64
KV_HEADS = 8
HD = 64
WINDOW = 128
TOPK = 4
EXP_DEV = 2


epsilon = 1e-05


def shifted(value, axis, steps):
    count = lax.axis_size(axis)
    initial, last = (max(0, -steps), min(count, count - steps))
    return lax.ppermute(value, axis, [(source, source + steps) for source in range(initial, last)])


def body(
    queries,
    keyvals,
    sinks,
    out_proj,
    residual,
    norm_gain,
    router_weight,
    route_ids,
    expert_in,
    expert_out,
):
    tokens_here = queries.shape[0]
    local_heads = queries.shape[1] // HD
    group_size = HEADS // KV_HEADS
    seq_devices = lax.axis_size("seq")
    experts_total = EXP_DEV * seq_devices
    capacity = 2 * tokens_here * TOPK // experts_total
    feature_share = residual.shape[1]
    panel_count = lax.axis_size("exp") // EXP_DEV
    mine = lax.axis_index("exp") // panel_count
    owner_mask = jnp.arange(EXP_DEV, dtype=jnp.int32) == mine
    weight_in = expert_in[0]
    weight_out = expert_out[0]
    head_owner = (
        lax.axis_index("exp") * local_heads + jnp.arange(local_heads, dtype=jnp.int32)
    ) // group_size
    kv_split = keyvals.reshape(tokens_here, 2, KV_HEADS, HD)
    chosen = jnp.take(kv_split, head_owner, axis=2).reshape(tokens_here, 2 * local_heads * HD)
    earlier = shifted(chosen, "seq", 1)
    key_values = jnp.concatenate([earlier, chosen], axis=0).reshape(
        WINDOW + tokens_here, 2, local_heads, HD
    )
    query_heads = queries.reshape(tokens_here, local_heads, HD)
    scores = (
        jnp.einsum(
            "thd,shd->hts", query_heads, key_values[:, 0], preferred_element_type=jnp.float32
        )
        * 0.125
    )
    query_pos = jnp.arange(tokens_here, dtype=jnp.int32)[:, None]
    key_pos = jnp.arange(WINDOW + tokens_here, dtype=jnp.int32)[None, :]
    offset = query_pos - key_pos + WINDOW
    allowed = (
        (offset >= 0) & (offset < WINDOW) & ((lax.axis_index("seq") > 0) | (key_pos >= WINDOW))
    )
    weights = jnp.where(allowed[None], jnp.exp(scores), jnp.float32(0.0))
    denominator = jnp.sum(weights, axis=2) + jnp.exp(sinks)[:, None]
    probabilities = (weights / denominator[:, :, None]).astype(jnp.bfloat16)
    attended = jnp.einsum(
        "hts,shd->thd", probabilities, key_values[:, 1], preferred_element_type=jnp.float32
    )
    attended = attended.astype(jnp.bfloat16).reshape(tokens_here, local_heads * HD)
    head_term = jnp.dot(attended, out_proj, preferred_element_type=jnp.float32)
    projected = lax.psum_scatter(
        head_term.astype(jnp.bfloat16), "exp", scatter_dimension=1, tiled=True
    ).astype(jnp.float32)
    hidden_state = residual.astype(jnp.float32) + projected
    scaled = hidden_state * norm_gain
    squares = lax.psum(jnp.sum(hidden_state * hidden_state, axis=1), "exp")
    factor = lax.rsqrt(squares / D + epsilon)
    logits = lax.psum(
        jnp.dot(scaled * factor[:, None], router_weight, precision=lax.Precision.HIGHEST), "exp"
    )
    normed = (scaled * factor[:, None]).astype(jnp.bfloat16)
    picked_logits = jnp.take_along_axis(logits, route_ids, axis=1)
    raised = jnp.exp(picked_logits)
    gate_values = raised / jnp.sum(raised, axis=1, keepdims=True)
    flat_ids = route_ids.reshape(tokens_here * TOPK)
    onehot = (flat_ids[:, None] == jnp.arange(experts_total, dtype=jnp.int32)[None, :]).astype(
        jnp.int32
    )
    running = jnp.cumsum(onehot, axis=0)
    slot_of = jnp.take_along_axis(running, flat_ids[:, None], axis=1)[:, 0] - 1
    target = flat_ids * capacity + slot_of
    repeated = jnp.repeat(normed, TOPK, axis=0)
    send_buffer = (
        jnp.zeros((experts_total * capacity, feature_share), jnp.bfloat16).at[target].set(repeated)
    )
    send_buffer = send_buffer.reshape(seq_devices, EXP_DEV, capacity, feature_share)
    received = lax.all_to_all(send_buffer, "seq", split_axis=0, concat_axis=0, tiled=True)
    piece_mine = lax.dynamic_index_in_dim(
        lax.all_gather(received, "exp", axis=3, tiled=True), mine, 1, keepdims=False
    )
    preact = jnp.einsum("scd,dgf->scgf", piece_mine, weight_in, preferred_element_type=jnp.float32)
    gate_part = preact[:, :, 0]
    up_part = preact[:, :, 1]
    activated = (gate_part * jax.nn.sigmoid(1.702 * gate_part) * (up_part + 1.0)).astype(
        jnp.bfloat16
    )
    unit_term = jnp.einsum("scf,fd->scd", activated, weight_out, preferred_element_type=jnp.float32)
    placed = jnp.where(owner_mask[None, :, None, None], unit_term[:, None], jnp.float32(0.0))
    summed = lax.psum_scatter(
        placed.astype(jnp.bfloat16), "exp", scatter_dimension=3, tiled=True
    ).astype(jnp.float32)
    returned = (
        lax.all_to_all(summed.astype(jnp.bfloat16), "seq", split_axis=0, concat_axis=0, tiled=True)
        .astype(summed.dtype)
        .reshape(experts_total * capacity, feature_share)
    )
    fetched = returned[target].reshape(tokens_here, TOPK, feature_share)
    mixture = jnp.sum(gate_values[:, :, None] * fetched, axis=1)
    return (hidden_state + mixture).astype(jnp.bfloat16)


def solution(mesh):
    return jax.shard_map(
        body,
        mesh=mesh,
        in_specs=(
            P("seq", "exp"),
            P("seq", None, None),
            P("exp"),
            P("exp", None),
            P("seq", "exp"),
            P("exp"),
            P("exp", None),
            P("seq", None),
            P(("seq", "exp"), None, None, None),
            P(("seq", "exp"), None, None),
        ),
        out_specs=P("seq", "exp"),
        check_vma=False,
    )
```

profile of v0, /device:TPU:64, one launch (start us, length us, event | category | flops | bytes accessed | tf_op | source)
XLA Modules:
  0.0 460.5 jit_solution(4834888659069381472)
XLA Ops:
  6.6 1.3 copy.48
  7.9 0.6 gather_fusion
  8.6 0.1 bitcast_select_fusion
  8.8 3.4 collective-permute-start
  12.3 0.8 copy.56
  13.2 0.1 broadcast_in_dim_reshape.4
  13.3 0.1 reshape.364
  13.4 1.0 copy.50
  14.4 0.7 exp.20
  15.1 1.2 reduce-window.6
  16.2 0.2 slice_reduce_fusion
  16.6 4.5 gather_fusion.3
  21.4 0.3 fusion.41
  21.8 0.2 convolution_convert_fusion.1
  22.0 0.6 copy-done.2
  22.6 0.5 convolution_convert_fusion
  23.1 25.3 %fusion = bf16[128,192]{0,1:T(8,128)(2,1)S(1)} fusion(bf16[128,2880]{0,1:T(8,128)(2,1)S(1)} %convolution_convert_fusion), kind=kCustom, calls=%all-reduce-scatter | all-reduce-scatter fusion | flops 393217 | bytes 787456
  48.5 3.0 collective-permute-start.1
  51.6 0.7 fusion.40
  52.9 0.9 collective-permute-done.1
  53.8 0.4 concatenate.14
  54.4 0.1 multiply_reduce_fusion.1
  54.5 25.4 %psum.14 = f32[128]{0:T(128)S(1)} all-reduce(f32[128]{0:T(128)S(1)} %multiply_reduce_fusion.1), channel_id=1, replica_groups=mesh['seq'=16,'exp'=16] {'exp'}, use_global_device_ids=true, to_apply=%region_3.4 | all-reduce | flops 128 | bytes 1024 | tf_op jit(solution)/shard_map/psum | solution.py:83
  80.1 0.2 reshape.407
  80.2 2.5 scatter_custom_fusion
  82.7 18.8 %all_to_all.10 = bf16[16,2,32,180]{3,2,1,0:T(8,128)(2,1)S(1)} all-to-all(bf16[16,2,32,180]{3,2,1,0:T(8,128)(2,1)S(1)} %bitcast.72), channel_id=1, replica_groups=mesh['seq'=16,'exp'=16] {'seq'}, dimensions={0} | all-to-all | bytes 737280 | tf_op jit(solution)/shard_map/all_to_all | solution.py:104
  101.6 2.2 copy.60
  103.8 0.2 all-reduce.5.cloned.1.call-start
  104.1 125.4 %all-gather.2.cloned.1.call-done = bf16[16,2,32,2880]{2,0,1,3:T(8,128)(2,1)} async-done(((bf16[16,2,32,180]{2,0,1,3:T(8,128)(2,1)}), bf16[16,2,32,2880]{2,0,1,3:T(8,128)(2,1)}) %all-gather.2.cloned.1.call-update) | async-done | bytes 5898256 | tf_op jit(solution)/shard_map/all_gather | solution.py:106
  229.5 10.5 %constant_dynamic-slice_fusion.2 = bf16[16,1,32,2880]{2,0,1,3:T(8,128)(2,1)} fusion(bf16[16,2,32,2880]{2,0,1,3:T(8,128)(2,1)} %all-gather.2.cloned.1.call-done, s32[]{:T(128)S(6)} %select_n.138), kind=kLoop, calls=%fused_computation.88 | loop fusion | bytes 5898244 | tf_op jit(solution)/shard_map/jit(dynamic_index_in_dim)/dynamic_slice | solution.py:105
  240.0 13.1 %copy.61 = bf16[16,1,32,2880]{3,2,0,1:T(8,128)(2,1)} copy(bf16[16,1,32,2880]{2,0,1,3:T(8,128)(2,1)} %constant_dynamic-slice_fusion.2) | data formatting | bytes 5898240 | tf_op jit(solution)/shard_map/jit(dynamic_index_in_dim)/dynamic_slice | solution.py:105
  253.1 5.8 %fusion.1 = f32[16,32,2,360]{3,1,2,0:T(8,128)S(1)} fusion(bf16[1,2880,2,360]{1,3,2,0:T(8,128)(2,1)} %param.18, bf16[16,1,32,2880]{3,2,0,1:T(8,128)(2,1)} %copy.61), kind=kOutput, calls=%fused_computation.6 | convolution fusion | flops 2123366400 | bytes 8570880 | tf_op jit(solution)/shard_map/scd,dgf->scgf/dot_general | solution.py:108
  258.9 1.8 fusion.4
  260.7 3.9 select_convert_fusion
  265.3 0.1 copy.53
  265.4 0.1 reshape.389
  265.5 0.3 fusion.27
  265.8 123.7 %all-reduce.5.cloned.1.call-done = bf16[16,2,32,2880]{3,2,1,0:T(8,128)(2,1)} async-done(((bf16[16,2,32,2880]{3,2,1,0:T(8,128)(2,1)}), bf16[16,2,32,2880]{3,2,1,0:T(8,128)(2,1)}) %all-reduce.5.cloned.1.call-update) | async-done | bytes 5898256
  389.5 2.2 constant_dynamic-slice_fusion.1
  391.7 6.9 %all-to-all-start.1 = ((bf16[16,2,32,180]{3,2,1,0:T(8,128)(2,1)}), bf16[16,2,32,180]{3,2,1,0:T(8,128)(2,1)}, u32[]{:S(2)}, u32[]{:S(2)}) async-start(bf16[16,2,32,180]{3,2,1,0:T(8,128)(2,1)} %constant_dynamic-slice_fusion.1), calls=%async_computation.1 | async-start | bytes 1048576 | tf_op jit(solution)/shard_map/all_to_all | solution.py:120
  398.6 45.1 %psum.15 = f32[128,32]{0,1:T(8,128)S(1)} all-reduce(f32[128,32]{0,1:T(8,128)S(1)} %fusion.27), channel_id=1, replica_groups=mesh['seq'=16,'exp'=16] {'exp'}, use_global_device_ids=true, to_apply=%region_4.5 | all-reduce | flops 4096 | bytes 32768 | tf_op jit(solution)/shard_map/psum | solution.py:85
  443.7 3.7 gather_fusion.2
  447.6 0.1 copy.55
  447.8 1.3 bitcast_convert_fusion
  449.1 2.2 gather_fusion.1
  451.3 1.2 reshape.370
  452.5 0.4 multiply_reduce_fusion
  452.9 0.7 copy.62
  (55 shorter events, 1.5 us)
Async XLA Ops:
  6.5 252.3 %copy-start = (bf16[1,360,2880]{2,1,0:T(8,128)(2,1)S(1)}, bf16[1,360,2880]{2,1,0:T(8,128)(2,1)}, u32[]{:S(2)}) copy-start(bf16[1,360,2880]{2,1,0:T(8,128)(2,1)} %param.19) | copy-start | bytes 6220804
  6.5 222.9 %all-gather.2.cloned.1.call-start = ((), (), s32[]{:S(2)}) async-start(), calls=%async_computation.2 | async-start | bytes 25067520 | tf_op jit(solution)/shard_map/all_gather | solution.py:106
  8.8 12.5 %collective-permute-start = (bf16[128,512]{0,1:T(8,128)(2,1)S(1)}, bf16[128,512]{0,1:T(8,128)(2,1)S(1)}, u32[]{:S(2)}, u32[]{:S(2)}) collective-permute-start(bf16[128,512]{0,1:T(8,128)(2,1)S(1)} %bitcast_select_fusion), channel_id=1, source_target_pairs={{0,16},{16,32},{32,48},{48,64},{64,80},{80,96},{96,112},{112,128},... | collective-permute-start | bytes 393224 | tf_op jit(solution)/shard_map/ppermute | solution.py:21
  21.2 1.4 copy-start.2
  21.3 30.1 %copy-start.3 = (bf16[128,180]{0,1:T(8,128)(2,1)S(1)}, bf16[128,180]{0,1:T(8,128)(2,1)}, u32[]{:S(2)}) copy-start(bf16[128,180]{0,1:T(8,128)(2,1)} %param.14) | copy-start | bytes 138244
  21.3 30.2 %copy-start.7 = (u32[256]{0:T(256)S(1)}, u32[256]{0:T(256)}, u32[]{:S(2)}) copy-start(u32[256]{0:T(256)} %constant.144) | copy-start | bytes 3076
  21.8 58.1 %copy-start.6 = (f32[180]{0:T(256)S(1)}, f32[180]{0:T(256)}, u32[]{:S(2)}) copy-start(f32[180]{0:T(256)} %param.15) | copy-start | bytes 2164
  48.5 5.4 %collective-permute-start.1 = (bf16[128,180]{0,1:T(8,128)(2,1)S(1)}, bf16[128,180]{0,1:T(8,128)(2,1)S(1)}, u32[]{:S(2)}, u32[]{:S(2)}) collective-permute-start(bf16[128,180]{0,1:T(8,128)(2,1)S(1)} %slice.39), channel_id=1, source_target_pairs={{0,1},{1,2},{2,3},{3,4},{4,5},{5,6},{6,7},{7,8},{8,9},{9,10},{10,1... | collective-permute-start | bytes 138248
  103.8 285.7 %all-reduce.5.cloned.1.call-start = ((), (), s32[]{:S(2)}) async-start(), calls=%async_computation.3 | async-start | bytes 12058624
  264.6 0.7 copy-start.4
  264.6 0.9 copy-start.5
  391.7 56.1 %all-to-all-start.1 = ((bf16[16,2,32,180]{3,2,1,0:T(8,128)(2,1)}), bf16[16,2,32,180]{3,2,1,0:T(8,128)(2,1)}, u32[]{:S(2)}, u32[]{:S(2)}) async-start(bf16[16,2,32,180]{3,2,1,0:T(8,128)(2,1)} %constant_dynamic-slice_fusion.1), calls=%async_computation.1 | async-start | bytes 1048576 | tf_op jit(solution)/shard_map/all_to_all | solution.py:120
  447.8 5.9 %copy-start.1 = (bf16[1,360,2880]{2,1,0:T(8,128)(2,1)S(1)}, bf16[1,360,2880]{2,1,0:T(8,128)(2,1)}, u32[]{:S(2)}) copy-start(bf16[1,360,2880]{2,1,0:T(8,128)(2,1)} %param.19) | copy-start | bytes 6220804
Sparse Core Ops, SparseCore 0:
  103.9 125.5 all-gather.1
  264.7 124.7 all-reduce.4
where the time goes:
time: 468 us; the launch traced here: 460 us
  waiting for transfers between devices  250 us (53%)
  blocking collectives  115 us (25%)
  local copies, waits for them, and re-layouts  50.6 us (11%)
  between operations  15.2 us (3%)
  starting transfers between devices  13.4 us (3%)
  matrix products  8.89 us (2%)
  other arithmetic  7.63 us (2%)
    all_gather x1, waiting for transfers between devices, body(): lax.all_gather(received, 'exp', axis=3, tiled=True)  125 us
    unnamed x4, waiting for transfers between devices  125 us
    psum x1, blocking collectives, body(): lax.psum(jnp.dot(scaled * factor[:, None], router_weight, precision=lax.P...  45.1 us
    psum x1, blocking collectives, body(): squares = lax.psum(jnp.sum(hidden_state * hidden_state, axis=1), 'exp')  25.4 us
    unnamed x1, blocking collectives  25.3 us
    dynamic_slice x2, local copies, waits for them, and re-layouts, body(): lax.dynamic_index_in_dim(lax.all_gather(received, 'exp', axis=3, tiled=Tr...  23.6 us
    all_to_all x1, blocking collectives, body(): lax.all_to_all(send_buffer, 'seq', split_axis=0, concat_axis=0, tiled=True)  18.8 us
  transfers between devices with their start and end apart: 5, of which 3 were waited for; matrix products, arithmetic and copies ran while one was open for 3% of the time, Pallas kernels for 0%

commit v1 on v0

v1 whole, which is shorter than its diff:
```python
import jax
import jax.numpy as jnp
from jax import lax
from jax.experimental import pallas as pl
from jax.experimental.pallas import tpu as pltpu
from jax.sharding import PartitionSpec as P

MESH = pl.DeviceIdType.MESH
F32, BF16 = jnp.float32, jnp.bfloat16
D = 2880
UNITS = 360
SHARE = 180
PAD = 192
PAIR = 2 * PAD
HALF = 8 * PAD
TOK = 128
CAP = 32
ROWS = 16 * CAP
EPS = 1e-05
STEPS = (
    (0, 0), (2, 2), (1, 2), (2, 1), (1, 1), (3, 3), (0, 1), (0, 3),
    (2, 3), (3, 2), (0, 2), (2, 0), (1, 3), (3, 1), (1, 0), (3, 0),
)
NT = (((1,), (1,)), ((), ()))


def nt(a, b):
    return lax.dot_general(a, b, NT, preferred_element_type=F32)


def nn(a, b):
    return jnp.dot(a, b, preferred_element_type=F32)


def kernel(
    q_ref, kv_ref, sink_ref, proj_hbm, res_ref, gain_ref, router_ref, route_ref, win_hbm, wout_hbm,
    out_ref,
    proj, stage, kvall, wide, codes, pick, part, sibsend, sibrecv, rsend, rrecv, hid, mine,
    diff, sel, weights, sqsend, sqrecv, lgsend, lgrecv, xg, dsend, x, gates, gthi, gtlo, ghi, glo,
    gacc, uacc, own, csend, crecv, ysend, y, macc, msend, mrecv,
    load_sem, halo_sem, sib_s, sib_r, rs_s, rs_r, sq_s, sq_r, lg_s, lg_r, ag_s, ag_r,
    d_s, d_r, f_s, f_r, c_s, c_r, y_s, y_r, m_s, m_r,
):
    s, e = lax.axis_index("seq"), lax.axis_index("exp")
    z, k = e // 2, lax.rem(e, 2)
    h = e // 8
    other = 1 - k
    sy, sx = s // 4, lax.rem(s, 4)
    ahead = [lax.rem(sy + dy, 4) * 4 + lax.rem(sx + dx, 4) for dy, dx in STEPS]
    behind = [lax.rem(sy + 4 - dy, 4) * 4 + lax.rem(sx + 4 - dx, 4) for dy, dx in STEPS]
    sibling = {"exp": 2 * z + other}
    zup = [lax.rem(z + d, 8) for d in range(8)]
    zdown = [lax.rem(z + 8 - d, 8) for d in range(8)]

    def remote(src, dst, send, recv, device):
        return pltpu.make_async_remote_copy(
            src_ref=src, dst_ref=dst, send_sem=send, recv_sem=recv, device_id=device, device_id_type=MESH
        )

    barrier = pltpu.get_barrier_semaphore()
    for d in range(1, 16):
        pl.semaphore_signal(barrier, inc=1, device_id={"seq": ahead[d]}, device_id_type=MESH)
        pl.semaphore_signal(barrier, inc=1, device_id={"exp": lax.rem(e + d, 16)}, device_id_type=MESH)
    load_proj = pltpu.make_async_copy(proj_hbm, proj, load_sem.at[0])
    load_in = pltpu.make_async_copy(win_hbm, stage.at[pl.ds(0, 2)], load_sem.at[1])
    load_out = pltpu.make_async_copy(wout_hbm, stage.at[2], load_sem.at[2])
    load_proj.start()
    load_in.start()
    load_out.start()
    kvall[TOK:, :] = kv_ref[...]
    pl.semaphore_wait(barrier, 30)

    halo = remote(kv_ref, kvall.at[pl.ds(0, TOK)], halo_sem.at[0], halo_sem.at[1], {"seq": lax.rem(s + 1, 16)})
    halo.start()

    expert = lax.broadcasted_iota(jnp.int32, (32, TOK), 0)
    named = route_ref[0:1, :] == expert
    for j in range(1, 4):
        named = named | (route_ref[j : j + 1, :] == expert)
    named = jnp.where(named, jnp.float32(1.0), jnp.float32(0.0))
    before = jnp.where(
        lax.broadcasted_iota(jnp.int32, (TOK, TOK), 0) < lax.broadcasted_iota(jnp.int32, (TOK, TOK), 1),
        jnp.float32(1.0), jnp.float32(0.0),
    ).astype(BF16)
    rank = nn(named.astype(BF16), before)
    codes[...] = jnp.where(named > 0.0, rank, jnp.float32(-1.0))
    row = lax.broadcasted_iota(jnp.int32, (CAP, TOK), 0).astype(F32)
    for d in range(16):
        code = codes[pl.ds(2 * ahead[d] + h, 1), :]
        pick[CAP * d : CAP * (d + 1), :] = jnp.where(code == row, jnp.float32(1.0), jnp.float32(0.0)).astype(BF16)
    weights[...] = jnp.zeros_like(weights)

    halo.wait_recv()
    kvf = kvall[...].astype(F32)
    turned = pltpu.roll(kvf, 64, 1)
    low = lax.broadcasted_iota(jnp.int32, (2 * TOK, TOK), 1) < 64
    zero = jnp.zeros_like(kvf)
    keys = [jnp.where(low, kvf, zero).astype(BF16), jnp.where(low, zero, turned).astype(BF16)]
    values = [jnp.where(low, turned, zero).astype(BF16), jnp.where(low, zero, kvf).astype(BF16)]
    qpos = lax.broadcasted_iota(jnp.int32, (TOK, 2 * TOK), 0)
    kpos = lax.broadcasted_iota(jnp.int32, (TOK, 2 * TOK), 1)
    offset = qpos - kpos + TOK
    allowed = (offset >= 0) & (offset < TOK) & (kpos >= jnp.where(s > 0, 0, TOK))
    for pair in range(2):
        query = q_ref[:, 128 * pair : 128 * (pair + 1)]
        total = None
        for side in range(2):
            head = 2 * pair + side
            score = nt(query, keys[side]) * 0.125
            weight = jnp.where(allowed, jnp.exp(score), jnp.float32(0.0))
            denominator = jnp.sum(weight, axis=1, keepdims=True) + jnp.exp(sink_ref[0:1, head : head + 1])
            term = nn((weight / denominator).astype(BF16), values[side])
            total = term if total is None else total + term
        wide[:, 128 * pair : 128 * (pair + 1)] = total.astype(BF16)

    load_proj.wait()
    attended = wide[...]

    def project(i, carry):
        r = pl.multiple_of(i * 576, 576)
        part[pl.ds(r, 576), :] = nt(proj[pl.ds(r, 576), :], attended)
        return carry

    lax.fori_loop(0, 5, project, 0)
    part[D : D + 16, :] = jnp.zeros((16, TOK), F32)
    order = (1, 2, 3, 4, 5, 6, 7, 0)
    first, second = [None] * 8, [None] * 8
    for d in order:
        sibsend[d] = part[pl.ds(SHARE * (2 * zup[d] + other), PAD), :].astype(BF16)
        first[d] = remote(sibsend.at[d], sibrecv.at[d], sib_s.at[d], sib_r.at[d], sibling)
        first[d].start()
    for d in order:
        first[d].wait_recv()
        pair_sum = part[pl.ds(SHARE * (2 * zup[d] + k), PAD), :] + sibrecv[d].astype(F32)
        if d == 0:
            mine[...] = pair_sum
        else:
            rsend[d] = pair_sum.astype(BF16)
            second[d] = remote(rsend.at[d], rrecv.at[d], rs_s.at[d], rs_r.at[d], {"exp": 2 * zup[d] + k})
            second[d].start()

    load_in.wait()
    load_out.wait()
    ji = lax.broadcasted_iota(jnp.int32, (2 * PAIR, PAIR), 1)
    di = lax.broadcasted_iota(jnp.int32, (2 * PAIR, PAIR), 0) - ji
    di = jnp.where(ji < SHARE, di, -9999)
    ji2 = (ji >= PAD) & (ji < PAD + SHARE)
    di2 = lax.broadcasted_iota(jnp.int32, (2 * PAIR, PAIR), 0) - ji - (2 * SHARE - PAD)
    diff[...] = jnp.where(ji2, di2, di)

    def spread(t, carry):
        q, p = t // 2, lax.rem(t, 2)
        start = 4 * SHARE * q + SHARE * p
        w0 = (start // 128) * 128
        sel[...] = jnp.where(diff[...] == start - w0, jnp.float32(1.0), jnp.float32(0.0)).astype(BF16)

        def matrix(m, c):
            block = stage[m, :, pl.ds(pl.multiple_of(w0, 128), 2 * PAIR)]
            weights[m, p, 0:UNITS, pl.ds(pl.multiple_of(q * PAIR, 128), PAIR)] = nn(block, sel[...]).astype(BF16)
            return c

        return lax.fori_loop(0, 3, matrix, carry)

    lax.fori_loop(0, 7, spread, 0)
    sel[...] = jnp.where(diff[...] == 36, jnp.float32(1.0), jnp.float32(0.0)).astype(BF16)

    def last(m, c):
        block = stage[m, :, 2304:D]
        weights[m, 1, 0:UNITS, 3 * PAIR : 4 * PAIR] = nn(block, sel[0:576, :]).astype(BF16)
        return c

    lax.fori_loop(0, 3, last, 0)

    total = mine[...]
    for d in range(1, 8):
        second[d].wait_recv()
        total = total + rrecv[d].astype(F32)
    hid[SHARE - 4 :, :] = jnp.zeros((PAD - SHARE + 4, TOK), F32)
    hid[0:SHARE, :] = res_ref[...].astype(F32) + total[0:SHARE, :]
    state = hid[...]
    sqsend[...] = jnp.broadcast_to(jnp.sum(state * state, axis=0, keepdims=True), (8, TOK))
    squares = [None] * 16
    for d in range(1, 16):
        device = {"exp": lax.rem(e + d, 16)}
        squares[d] = remote(sqsend, sqrecv.at[d], sq_s.at[d], sq_r.at[d], device)
        squares[d].start()
    diagonal = lax.broadcasted_iota(jnp.int32, (PAD, SHARE), 0) == lax.broadcasted_iota(jnp.int32, (PAD, SHARE), 1)
    gain = jnp.sum(jnp.where(diagonal, gain_ref[...], jnp.float32(0.0)), axis=1, keepdims=True)
    scaled = state * gain
    xg[z] = scaled.astype(BF16)
    gather = [None] * 8
    for d in range(1, 8):
        gather[d] = remote(xg.at[z], xg.at[z], ag_s.at[d], ag_r.at[d], {"exp": 2 * zup[d] + k})
        gather[d].start()
    lgsend[...] = jnp.dot(
        router_ref[...], scaled[0:SHARE, :], precision=lax.Precision.HIGHEST, preferred_element_type=F32
    )
    logit_copies = [None] * 16
    for d in range(1, 16):
        device = {"exp": lax.rem(e + d, 16)}
        logit_copies[d] = remote(lgsend, lgrecv.at[d], lg_s.at[d], lg_r.at[d], device)
        logit_copies[d].start()
    square = sqsend[0:1, :]
    for d in range(1, 16):
        squares[d].wait_recv()
        square = square + sqrecv[d, 0:1, :]
    factor = lax.rsqrt(square / D + EPS)

    for d in range(1, 8):
        slot = zdown[d]
        remote(xg.at[slot], xg.at[slot], ag_s.at[d], ag_r.at[d], {"exp": 2 * zup[d] + k}).wait_recv()
    sends = [None] * 16
    for g in range(4):
        r = slice(TOK * g, TOK * (g + 1))
        chosen = pick[r, :]
        scale = jnp.sum(chosen.astype(F32) * factor, axis=1, keepdims=True)
        for q in range(4):
            features = xg[2 * q : 2 * q + 2].reshape(PAIR, TOK)
            dsend[r, PAIR * q : PAIR * (q + 1)] = (nt(chosen, features) * scale).astype(BF16)
        for d in range(4 * g, 4 * g + 4):
            if d == 0:
                x[k, 0:CAP, :] = dsend[0:CAP, :]
            else:
                sends[d] = remote(
                    dsend.at[pl.ds(CAP * d, CAP)], x.at[k, pl.ds(CAP * d, CAP)], d_s.at[d], d_r.at[d], {"seq": ahead[d]}
                )
                sends[d].start()

    logits = lgsend[...]
    for d in range(1, 16):
        logit_copies[d].wait_recv()
        logits = logits + lgrecv[d]
    raised = jnp.where(named > 0.0, jnp.exp(logits * factor), jnp.float32(0.0))
    gates[...] = raised / jnp.sum(raised, axis=0, keepdims=True)
    for d in range(16):
        r = slice(CAP * d, CAP * (d + 1))
        gate = gates[pl.ds(2 * ahead[d] + h, 1), :] * pick[r, :].astype(F32)
        gthi[r, :] = gate.astype(BF16)
        gtlo[r, :] = (gate - gate.astype(BF16).astype(F32)).astype(BF16)
    unit = jnp.where(
        lax.broadcasted_iota(jnp.int32, (TOK, TOK), 0) == lax.broadcasted_iota(jnp.int32, (TOK, TOK), 1),
        jnp.float32(1.0), jnp.float32(0.0),
    ).astype(BF16)
    ghi[...] = nt(unit, gthi[...]).astype(BF16)
    glo[...] = nt(unit, gtlo[...]).astype(BF16)

    backs = [None] * 16
    forwards = [None] * 16
    pairs = [None] * 2
    for g in range(2):
        base = 256 * g
        r = slice(base, base + 256)
        for d in range(8 * g, 8 * g + 8):
            piece = pl.ds(CAP * d, CAP)
            if d > 0:
                sends[d].wait_recv()
            forwards[d] = remote(x.at[k, piece], x.at[k, piece], f_s.at[d], f_r.at[d], sibling)
            forwards[d].start()
        gacc[...] = nt(x[k, r, :], weights[0, k])
        uacc[...] = nt(x[k, r, :], weights[1, k])
        for d in range(8 * g, 8 * g + 8):
            piece = pl.ds(CAP * d, CAP)
            remote(x.at[other, piece], x.at[other, piece], f_s.at[d], f_r.at[d], sibling).wait_recv()
        gate = gacc[...] + nt(x[other, r, :], weights[0, other])
        up = uacc[...] + nt(x[other, r, :], weights[1, other])
        activated = (gate * jax.nn.sigmoid(1.702 * gate) * (up + 1.0)).astype(BF16)
        csend[r, :] = nn(activated, weights[2, other]).astype(BF16)
        pairs[g] = remote(csend.at[pl.ds(base, 256)], crecv.at[pl.ds(base, 256)], c_s.at[g], c_r.at[g], sibling)
        pairs[g].start()
        own[...] = nn(activated, weights[2, k])
        pairs[g].wait_recv()
        for d in range(8 * g, 8 * g + 8):
            b = slice(CAP * d, CAP * (d + 1))
            block = (own[CAP * d - base : CAP * (d + 1) - base, :] + crecv[b, :].astype(F32)).astype(BF16)
            if d == 0:
                y[b, :] = block
            else:
                ysend[b, :] = block
                piece = pl.ds(CAP * d, CAP)
                backs[d] = remote(ysend.at[piece], y.at[piece], y_s.at[d], y_r.at[d], {"seq": behind[d]})
                backs[d].start()

    for g in range(2):
        r = slice(256 * g, 256 * (g + 1))
        for d in range(8 * g, 8 * g + 8):
            if d > 0:
                backs[d].wait_recv()
        term = nn(ghi[:, r], y[r, :]) + nn(glo[:, r], y[r, :])
        if g == 0:
            macc[...] = term
        else:
            macc[...] = macc[...] + term
    unit = jnp.where(
        lax.broadcasted_iota(jnp.int32, (PAIR, PAIR), 0) == lax.broadcasted_iota(jnp.int32, (PAIR, PAIR), 1),
        jnp.float32(1.0), jnp.float32(0.0),
    ).astype(BF16)
    for q in range(4):
        turned = nt(unit, macc[:, PAIR * q : PAIR * (q + 1)].astype(BF16))
        msend[2 * q : 2 * q + 2] = turned.astype(BF16).reshape(2, PAD, TOK)
    finals = [None] * 8
    for d in range(1, 8):
        finals[d] = remote(msend.at[zup[d]], mrecv.at[d], m_s.at[d], m_r.at[d], {"exp": 2 * zup[d] + k})
        finals[d].start()
    total = hid[...] + msend[z].astype(F32)
    for d in range(1, 8):
        finals[d].wait_recv()
        total = total + mrecv[d].astype(F32)
    out_ref[...] = total[0:SHARE, :].astype(BF16)

    halo.wait_send()
    for d in range(8):
        first[d].wait_send()
    for d in range(1, 8):
        second[d].wait_send()
        gather[d].wait_send()
        finals[d].wait_send()
    for d in range(1, 16):
        squares[d].wait_send()
        logit_copies[d].wait_send()
        sends[d].wait_send()
        backs[d].wait_send()
    for d in range(16):
        forwards[d].wait_send()
    for g in range(2):
        pairs[g].wait_send()


def vmem(*shape, dtype=BF16):
    return pltpu.VMEM(shape, dtype)


def body(
    queries, keyvals, sinks, out_proj, residual, norm_gain, router_weight, route_ids, expert_in, expert_out
):
    z = lax.axis_index("exp") // 2
    kv = lax.dynamic_slice(keyvals, (0, 0, 64 * z), (TOK, 2, 64)).reshape(TOK, TOK)
    local = pl.BlockSpec(memory_space=pltpu.VMEM)
    far = pl.BlockSpec(memory_space=pltpu.HBM)
    sems = lambda n: pltpu.SemaphoreType.DMA((n,))
    mixed = pl.pallas_call(
        kernel,
        out_shape=jax.ShapeDtypeStruct((SHARE, TOK), BF16),
        in_specs=[local, local, local, far, local, local, local, local, far, far],
        out_specs=local,
        scratch_shapes=[
            vmem(D, 256),
            vmem(3, UNITS, D),
            vmem(2 * TOK, TOK),
            vmem(TOK, 256),
            vmem(32, TOK, dtype=F32),
            vmem(ROWS, TOK),
            vmem(D + 16, TOK, dtype=F32),
            vmem(8, PAD, TOK),
            vmem(8, PAD, TOK),
            vmem(8, PAD, TOK),
            vmem(8, PAD, TOK),
            vmem(PAD, TOK, dtype=F32),
            vmem(PAD, TOK, dtype=F32),
            vmem(2 * PAIR, PAIR, dtype=jnp.int32),
            vmem(2 * PAIR, PAIR),
            vmem(3, 2, PAIR, HALF),
            vmem(8, TOK, dtype=F32),
            vmem(16, 8, TOK, dtype=F32),
            vmem(32, TOK, dtype=F32),
            vmem(16, 32, TOK, dtype=F32),
            vmem(8, PAD, TOK),
            vmem(ROWS, HALF),
            vmem(2, ROWS, HALF),
            vmem(32, TOK, dtype=F32),
            vmem(ROWS, TOK),
            vmem(ROWS, TOK),
            vmem(TOK, ROWS),
            vmem(TOK, ROWS),
            vmem(256, PAIR, dtype=F32),
            vmem(256, PAIR, dtype=F32),
            vmem(256, HALF, dtype=F32),
            vmem(ROWS, HALF),
            vmem(ROWS, HALF),
            vmem(ROWS, HALF),
            vmem(ROWS, HALF),
            vmem(TOK, HALF, dtype=F32),
            vmem(8, PAD, TOK),
            vmem(8, PAD, TOK),
            sems(3), sems(2), sems(8), sems(8), sems(8), sems(8), sems(16), sems(16), sems(16), sems(16),
            sems(8), sems(8), sems(16), sems(16), sems(16), sems(16), sems(2), sems(2), sems(16), sems(16),
            sems(8), sems(8),
        ],
        compiler_params=pltpu.CompilerParams(
            collective_id=0, has_side_effects=True, vmem_limit_bytes=56 * 2**20
        ),
        name="layer",
    )(
        queries,
        kv,
        sinks.reshape(1, 4),
        out_proj.T,
        residual.T,
        norm_gain.reshape(1, SHARE),
        router_weight.T,
        route_ids.T,
        jnp.transpose(expert_in[0], (1, 2, 0)),
        expert_out[0],
    )
    return mixed.T


def solution(mesh):
    return jax.shard_map(
        body,
        mesh=mesh,
        in_specs=(
            P("seq", "exp"),
            P("seq", None, None),
            P("exp"),
            P("exp", None),
            P("seq", "exp"),
            P("exp"),
            P("exp", None),
            P("seq", None),
            P(("seq", "exp"), None, None, None),
            P(("seq", "exp"), None, None),
        ),
        out_specs=P("seq", "exp"),
        check_vma=False,
    )
```

time: 468 us -> 104 us (0.22); the launches traced: 460 us -> 103 us
  waiting for transfers between devices: 250 us -> 0 us
  blocking collectives: 115 us -> 0 us
  Pallas kernels: 0 us -> 99.4 us
  local copies, waits for them, and re-layouts: 50.6 us -> 3.33 us
  between operations: 15.2 us -> 0.03 us
  starting transfers between devices: 13.4 us -> 0 us
  matrix products: 8.89 us -> 0 us
  other arithmetic: 7.63 us -> 0 us
    all_gather x1 -> x0, waiting for transfers between devices: 125 us -> none  [body(): lax.all_gather(received, 'exp', axis=3, tiled=True)]
    unnamed x4 -> x0, waiting for transfers between devices: 125 us -> none
    pallas_call x0 -> x1, Pallas kernels: none -> 99.4 us  [body(): pl.pallas_call(kernel, out_shape=jax.ShapeDtypeStruct((SHARE, TOK), BF16)...]
    psum x2 -> x0, blocking collectives: 70.5 us -> none  [the longest x1 45.1 us: body(): lax.psum(jnp.dot(scaled * factor[:, None], router_weight, precision=lax.P...]
    unnamed x1 -> x0, blocking collectives: 25.3 us -> none
    dynamic_slice x2 -> x1, local copies, waits for them, and re-layouts: 23.6 us -> 0.14 us  [body(): lax.dynamic_slice(keyvals, (0, 0, 64 * z), (TOK, 2, 64)).reshape(TOK, TOK)]
    all_to_all x1 -> x0, blocking collectives: 18.8 us -> none  [body(): lax.all_to_all(send_buffer, 'seq', split_axis=0, concat_axis=0, tiled=True)]
    gather x9 -> x0, local copies, waits for them, and re-layouts: 11.5 us -> none  [the longest x1 4.55 us: body(): slot_of = jnp.take_along_axis(running, flat_ids[:, None], axis=1)[:, 0] - 1]
  transfers between devices with their start and end apart: 5 -> 0, of which waited for: 3 -> 0; matrix products, arithmetic and copies ran while one was open for 3% -> 0% of each run, Pallas kernels for 0% -> 0%
where the time goes in v1:
time: 104 us; the launch traced here: 103 us
  Pallas kernels  99.4 us (96%)
  local copies, waits for them, and re-layouts  3.33 us (3%)
    pallas_call x1, Pallas kernels, body(): pl.pallas_call(kernel, out_shape=jax.ShapeDtypeStruct((SHARE, TOK), BF16)...  99.4 us
    unnamed x4, local copies, waits for them, and re-layouts  2.46 us

profile of v1, /device:TPU:64, one launch (start us, length us, event | category | flops | bytes accessed | tf_op | source)
XLA Modules:
  0.0 102.8 jit_solution(11210089406306681533)
XLA Ops:
  0.0 0.0 copy-start
  0.0 0.9 copy-done
  1.0 0.1 constant_dynamic-slice_fusion
  1.1 0.1 copy.13
  1.2 0.7 copy.12.kv_ref
  1.9 99.4 %layer.1 = bf16[180,128]{1,0:T(8,128)(2,1)} custom-call(bf16[128,256]{1,0:T(8,128)(2,1)} %q_ref.1, bf16[128,128]{1,0:T(8,128)(2,1)} %copy.12.kv_ref, f32[1,4]{1,0:T(1,128)} %bitcast.21, bf16[2880,256]{1,0:T(8,128)(2,1)} %bitcast.14, bf16[180,128]{1,0:T(8,128)(2,1)} %bitcast.17, f32[1,180]{1,0:T(1,128)} %bitcast.20, f32[32,180]{1,0:T(8,128)} %bitcast.18, ...), custom_call_target="tpu_custom_call" | custom-call | tf_op jit(solution)/shard_map/layer/pallas_call | solution.py:340
  101.4 1.4 %copy.15 = bf16[128,180]{0,1:T(8,128)(2,1)} copy(bf16[128,180]{0,1:T(8,128)(2,1)} %bitcast.15) | data formatting | bytes 92160
Async XLA Ops:
  0.0 1.0 copy-start

commit v2 on v1

v2 whole, which is shorter than its diff:
```python
import jax
import jax.numpy as jnp
from jax import lax
from jax.experimental import pallas as pl
from jax.experimental.pallas import tpu as pltpu
from jax.sharding import PartitionSpec as P

MESH = pl.DeviceIdType.MESH
F32, BF16 = jnp.float32, jnp.bfloat16
D = 2880
UNITS = 360
SHARE = 180
PAD = 192
PAIR = 2 * PAD
HALF = 8 * PAD
TOK = 128
CAP = 32
ROWS = 16 * CAP
EPS = 1e-05
STEPS = (
    (0, 0), (2, 2), (1, 2), (3, 2), (2, 1), (2, 3), (1, 1), (3, 3),
    (1, 3), (3, 1), (0, 2), (2, 0), (0, 1), (1, 0), (0, 3), (3, 0),
)
NT = (((1,), (1,)), ((), ()))


def nt(a, b):
    return lax.dot_general(a, b, NT, preferred_element_type=F32)


def nn(a, b):
    return jnp.dot(a, b, preferred_element_type=F32)


def kernel(
    q_ref, kv_ref, sink_ref, proj_hbm, res_ref, gain_ref, router_ref, route_ref, win_hbm, wout_hbm,
    out_ref,
    proj, stage, kvall, wide, codes, pick, part, sibsend, sibrecv, rsend, rrecv, hid, mine,
    diff, sel, weights, sqsend, sqrecv, lgsend, lgsib, lgsum, lgrecv, xg, esend, ssend, x, gates, gthi, gtlo, ghi, glo,
    gacc, uacc, owns, owne, csend, crecv, psend, precv, yssend, yesend, ys, ye, maccs, macce, msends, msende, mrecv,
    load_sem, halo_sem, sib_s, sib_r, rs_s, rs_r, sq_s, sq_r, lg_s, lg_r, ag_s, ag_r,
    de_s, de_r, ds_s, ds_r, pf_s, pf_r, f_s, f_r, c_s, c_r, p_s, p_r, ys_s, ys_r, ye_s, ye_r, m_s, m_r,
):
    s, e = lax.axis_index("seq"), lax.axis_index("exp")
    z, k = e // 2, lax.rem(e, 2)
    h, b, mid = e // 8, lax.rem(z, 2), lax.rem(z // 2, 2)
    other = 1 - k
    sy, sx = s // 4, lax.rem(s, 4)
    ahead = [lax.rem(sy + dy, 4) * 4 + lax.rem(sx + dx, 4) for dy, dx in STEPS]
    behind = [lax.rem(sy + 4 - dy, 4) * 4 + lax.rem(sx + 4 - dx, 4) for dy, dx in STEPS]
    sibling = {"exp": 2 * z + other}
    zup = [lax.rem(z + d, 8) for d in range(8)]
    mate = z + 1 - 2 * b
    partner = {"exp": 2 * mate + k}
    far_half = 4 * (1 - h)
    group = 2 * h + b
    lane_e = pl.multiple_of(PAIR * group, 128)
    lane_p = pl.multiple_of(PAIR * (2 * h + 1 - b), 128)
    lane_s = pl.multiple_of(2 * PAIR * (1 - h), 128)
    lane_o = pl.multiple_of(2 * PAIR * h, 128)

    def remote(src, dst, send, recv, device):
        return pltpu.make_async_remote_copy(
            src_ref=src, dst_ref=dst, send_sem=send, recv_sem=recv, device_id=device, device_id_type=MESH
        )

    barrier = pltpu.get_barrier_semaphore()
    for d in range(1, 16):
        pl.semaphore_signal(barrier, inc=1, device_id={"seq": ahead[d]}, device_id_type=MESH)
        pl.semaphore_signal(barrier, inc=1, device_id={"exp": lax.rem(e + d, 16)}, device_id_type=MESH)
    load_proj = pltpu.make_async_copy(proj_hbm, proj, load_sem.at[0])
    load_in = pltpu.make_async_copy(win_hbm, stage.at[pl.ds(0, 2)], load_sem.at[1])
    load_out = pltpu.make_async_copy(wout_hbm, stage.at[2], load_sem.at[2])
    load_proj.start()
    load_in.start()
    load_out.start()
    kvall[TOK:, :] = kv_ref[...]

    expert = lax.broadcasted_iota(jnp.int32, (32, TOK), 0)
    named = route_ref[0:1, :] == expert
    for j in range(1, 4):
        named = named | (route_ref[j : j + 1, :] == expert)
    named = jnp.where(named, jnp.float32(1.0), jnp.float32(0.0))
    before = jnp.where(
        lax.broadcasted_iota(jnp.int32, (TOK, TOK), 0) < lax.broadcasted_iota(jnp.int32, (TOK, TOK), 1),
        jnp.float32(1.0), jnp.float32(0.0),
    ).astype(BF16)
    rank = nn(named.astype(BF16), before)
    codes[...] = jnp.where(named > 0.0, rank, jnp.float32(-1.0))
    row = lax.broadcasted_iota(jnp.int32, (CAP, TOK), 0).astype(F32)
    for d in range(16):
        code = codes[pl.ds(2 * ahead[d] + h, 1), :]
        pick[CAP * d : CAP * (d + 1), :] = jnp.where(code == row, jnp.float32(1.0), jnp.float32(0.0)).astype(BF16)

    pl.semaphore_wait(barrier, 30)
    halo = remote(kv_ref, kvall.at[pl.ds(0, TOK)], halo_sem.at[0], halo_sem.at[1], {"seq": lax.rem(s + 1, 16)})
    halo.start()
    weights[...] = jnp.zeros_like(weights)

    low = lax.broadcasted_iota(jnp.int32, (TOK, TOK), 1) < 64

    def sides(ref_part):
        kvf = ref_part.astype(F32)
        turned = pltpu.roll(kvf, 64, 1)
        zero = jnp.zeros_like(kvf)
        keys = [jnp.where(low, kvf, zero).astype(BF16), jnp.where(low, zero, turned).astype(BF16)]
        values = [jnp.where(low, turned, zero).astype(BF16), jnp.where(low, zero, kvf).astype(BF16)]
        return keys, values

    qpos = lax.broadcasted_iota(jnp.int32, (TOK, TOK), 0)
    kpos = lax.broadcasted_iota(jnp.int32, (TOK, TOK), 1)
    keys, values = sides(kvall[TOK:, :])
    new = []
    for head in range(4):
        query = q_ref[:, 128 * (head // 2) : 128 * (head // 2 + 1)]
        score = nt(query, keys[head % 2]) * 0.125
        new.append(jnp.where(kpos <= qpos, jnp.exp(score), jnp.float32(0.0)))
    new_values = values
    halo.wait_recv()
    keys, values = sides(kvall[0:TOK, :])
    allowed = kpos > qpos + jnp.where(s > 0, 0, TOK)
    for pair in range(2):
        query = q_ref[:, 128 * pair : 128 * (pair + 1)]
        total = None
        for side in range(2):
            head = 2 * pair + side
            score = nt(query, keys[side]) * 0.125
            weight = jnp.where(allowed, jnp.exp(score), jnp.float32(0.0))
            denominator = jnp.sum(weight + new[head], axis=1, keepdims=True) + jnp.exp(
                sink_ref[0:1, head : head + 1]
            )
            scale = 1.0 / denominator
            term = nn((weight * scale).astype(BF16), values[side])
            term = term + nn((new[head] * scale).astype(BF16), new_values[side])
            total = term if total is None else total + term
        wide[:, 128 * pair : 128 * (pair + 1)] = total.astype(BF16)

    load_proj.wait()
    attended = wide[...]

    def project(i, carry):
        r = pl.multiple_of(i * 576, 576)
        part[pl.ds(r, 576), :] = nt(proj[pl.ds(r, 576), :], attended)
        return carry

    lax.fori_loop(0, 5, project, 0)
    part[D : D + 16, :] = jnp.zeros((16, TOK), F32)
    order = (4, 3, 5, 2, 6, 1, 7, 0)
    first, second = [None] * 8, [None] * 8
    for d in order:
        sibsend[d] = part[pl.ds(SHARE * (2 * zup[d] + other), PAD), :].astype(BF16)
        first[d] = remote(sibsend.at[d], sibrecv.at[d], sib_s.at[d], sib_r.at[d], sibling)
        first[d].start()
    for d in order:
        first[d].wait_recv()
        pair_sum = part[pl.ds(SHARE * (2 * zup[d] + k), PAD), :] + sibrecv[d].astype(F32)
        if d == 0:
            mine[...] = pair_sum
        else:
            rsend[d] = pair_sum.astype(BF16)
            second[d] = remote(rsend.at[d], rrecv.at[d], rs_s.at[d], rs_r.at[d], {"exp": 2 * zup[d] + k})
            second[d].start()

    load_in.wait()
    ji = lax.broadcasted_iota(jnp.int32, (2 * PAIR, PAIR), 1)
    di = lax.broadcasted_iota(jnp.int32, (2 * PAIR, PAIR), 0) - ji
    di = jnp.where(ji < SHARE, di, -9999)
    ji2 = (ji >= PAD) & (ji < PAD + SHARE)
    di2 = lax.broadcasted_iota(jnp.int32, (2 * PAIR, PAIR), 0) - ji - (2 * SHARE - PAD)
    diff[...] = jnp.where(ji2, di2, di)

    def spread(first_matrix, count):
        def block(t, carry):
            q, p = t // 2, lax.rem(t, 2)
            start = 4 * SHARE * q + SHARE * p
            w0 = (start // 128) * 128
            sel[...] = jnp.where(diff[...] == start - w0, jnp.float32(1.0), jnp.float32(0.0)).astype(BF16)

            def matrix(m, c):
                window = stage[m, :, pl.ds(pl.multiple_of(w0, 128), 2 * PAIR)]
                lanes = pl.ds(pl.multiple_of(q * PAIR, 128), PAIR)
                weights[m, p, 0:UNITS, lanes] = nn(window, sel[...]).astype(BF16)
                return c

            return lax.fori_loop(first_matrix, first_matrix + count, matrix, carry)

        def last(m, c):
            window = stage[m, :, 2304:D]
            weights[m, 1, 0:UNITS, 3 * PAIR : 4 * PAIR] = nn(window, sel[0:576, :]).astype(BF16)
            return c

        lax.fori_loop(0, 7, block, 0)
        sel[...] = jnp.where(diff[...] == 36, jnp.float32(1.0), jnp.float32(0.0)).astype(BF16)
        lax.fori_loop(first_matrix, first_matrix + count, last, 0)

    spread(0, 2)

    total = mine[...]
    for d in (1, 7, 2, 6, 3, 5, 4):
        second[d].wait_recv()
        total = total + rrecv[d].astype(F32)
    hid[SHARE - 4 :, :] = jnp.zeros((PAD - SHARE + 4, TOK), F32)
    hid[0:SHARE, :] = res_ref[...].astype(F32) + total[0:SHARE, :]
    state = hid[...]
    diagonal = lax.broadcasted_iota(jnp.int32, (PAD, SHARE), 0) == lax.broadcasted_iota(jnp.int32, (PAD, SHARE), 1)
    gain = jnp.sum(jnp.where(diagonal, gain_ref[...], jnp.float32(0.0)), axis=1, keepdims=True)
    scaled = state * gain
    xg[z] = scaled.astype(BF16)
    sqsend[...] = jnp.sum(state * state, axis=0, keepdims=True)
    gather = [
        remote(xg.at[z], xg.at[z], ag_s.at[0], ag_r.at[0], partner),
        remote(xg.at[z], xg.at[z], ag_s.at[1], ag_r.at[1 + b], {"exp": 2 * (4 * h + 2 - mid) + k}),
    ]
    for j in range(4):
        device = {"exp": 2 * (far_half + j) + k}
        gather.append(remote(xg.at[z], xg.at[z], ag_s.at[2 + j], ag_r.at[3 + lax.rem(z, 4)], device))
    gather[0].start()
    gather[1].start()
    squares = [None] * 16
    for d in range(1, 16):
        device = {"exp": lax.rem(e + d, 16)}
        squares[d] = remote(sqsend, sqrecv.at[d], sq_s.at[d], sq_r.at[d], device)
        squares[d].start()
    for j in range(4):
        gather[2 + j].start()
    lgsend[...] = jnp.dot(
        router_ref[...], scaled[0:SHARE, :], precision=lax.Precision.HIGHEST, preferred_element_type=F32
    )
    logit_copies = [remote(lgsend, lgsib, lg_s.at[0], lg_r.at[0], sibling)]
    logit_copies[0].start()
    def arrived(slot, sem):
        remote(xg.at[slot], xg.at[slot], ag_s.at[0], ag_r.at[sem], partner).wait_recv()

    arrived(mate, 0)

    @pl.when(b != mid)
    def _():
        arrived(4 * h + 2 * (1 - mid), 1)
        arrived(4 * h + 2 * (1 - mid) + 1, 2)

    to_e, to_s = [None] * 16, [None] * 16
    features = xg[pl.ds(2 * group, 2)].reshape(PAIR, TOK)
    for g in range(4):
        r = slice(TOK * g, TOK * (g + 1))
        chosen = pick[r, :]
        esend[r, :] = nt(chosen, features).astype(BF16)
        for d in range(4 * g, 4 * g + 4):
            if d == 0:
                x[k, 0:CAP, pl.ds(lane_e, PAIR)] = esend[0:CAP, :]
            else:
                piece = pl.ds(CAP * d, CAP)
                target = x.at[k, piece, pl.ds(lane_e, PAIR)]
                to_e[d] = remote(esend.at[piece], target, de_s.at[d], de_r.at[d], {"seq": ahead[d]})
                to_e[d].start()

    passed, forwards = [None] * 4, [None] * 12

    def pass_on(g):
        for d in range(4 * g, 4 * g + 4):
            if d > 0:
                to_e[d].wait_recv()
        block = x.at[k, pl.ds(TOK * g, TOK), pl.ds(lane_e, PAIR)]
        passed[g] = remote(block, block, pf_s.at[g], pf_r.at[g], partner)
        passed[g].start()
        forwards[g] = remote(block, block, f_s.at[g], f_r.at[g], sibling)
        forwards[g].start()

    pass_on(0)
    pass_on(1)
    for j in range(4):
        arrived(far_half + j, 3 + j)
    square = sqsend[...]
    for d in range(1, 16):
        squares[d].wait_recv()
        square = square + sqrecv[d]
    factor = lax.rsqrt(square / D + EPS)
    high = factor.astype(BF16).astype(F32)
    ti = lax.broadcasted_iota(jnp.int32, (16, TOK), 0)
    tail = xg[far_half, PAD - 16 :, :].astype(F32)
    tail = jnp.where(ti == 4, high, jnp.where(ti == 5, factor - high, tail))
    xg[far_half, PAD - 16 :, :] = tail.astype(BF16)
    for g in range(4):
        r = slice(TOK * g, TOK * (g + 1))
        for q in range(2):
            features = xg[pl.ds(far_half + 2 * q, 2)].reshape(PAIR, TOK)
            ssend[r, PAIR * q : PAIR * (q + 1)] = nt(pick[r, :], features).astype(BF16)
        for d in range(4 * g, 4 * g + 4):
            if d == 0:
                x[k, 0:CAP, pl.ds(lane_s, 2 * PAIR)] = ssend[0:CAP, :]
            else:
                piece = pl.ds(CAP * d, CAP)
                target = x.at[k, piece, pl.ds(lane_s, 2 * PAIR)]
                to_s[d] = remote(ssend.at[piece], target, ds_s.at[d], ds_r.at[d], {"seq": ahead[d]})
                to_s[d].start()
    pass_on(2)
    pass_on(3)

    logit_copies[0].wait_recv()
    lgsum[...] = lgsend[...] + lgsib[...]
    for d in range(1, 8):
        device = {"exp": 2 * zup[d] + k}
        logit_copies.append(remote(lgsum, lgrecv.at[d], lg_s.at[d], lg_r.at[d], device))
        logit_copies[d].start()
    unit = jnp.where(
        lax.broadcasted_iota(jnp.int32, (TOK, TOK), 0) == lax.broadcasted_iota(jnp.int32, (TOK, TOK), 1),
        jnp.float32(1.0), jnp.float32(0.0),
    ).astype(BF16)

    load_out.wait()
    spread(2, 1)

    def make_gates():
        logits = lgsum[...]
        for d in range(1, 8):
            logit_copies[d].wait_recv()
            logits = logits + lgrecv[d]
        raised = jnp.where(named > 0.0, jnp.exp(logits * factor), jnp.float32(0.0))
        gates[...] = raised / jnp.sum(raised, axis=0, keepdims=True)
        for d in range(16):
            r = slice(CAP * d, CAP * (d + 1))
            gate = gates[pl.ds(2 * ahead[d] + h, 1), :] * pick[r, :].astype(F32)
            gthi[r, :] = gate.astype(BF16)
            gtlo[r, :] = (gate - gate.astype(BF16).astype(F32)).astype(BF16)
        ghi[...] = nt(unit, gthi[...]).astype(BF16)
        glo[...] = nt(unit, gtlo[...]).astype(BF16)

    back_s, back_e, pairs, swaps = [None] * 16, [None] * 16, [None] * 4, [None] * 4

    def finish_group(g):
        for d in range(8 * g, 8 * g + 8):
            if d % 4 == 0:
                swaps[d // 4].wait_recv()
            blk = slice(CAP * d, CAP * (d + 1))
            block = owne[blk, pl.ds(pl.multiple_of(PAIR * b, 128), PAIR)] + precv[blk, :].astype(F32)
            if d == 0:
                ye[blk, :] = block.astype(BF16)
            else:
                yesend[blk, :] = block.astype(BF16)
                piece = pl.ds(CAP * d, CAP)
                back_e[d] = remote(yesend.at[piece], ye.at[piece], ye_s.at[d], ye_r.at[d], {"seq": behind[d]})
                back_e[d].start()

    def sum_shared(g):
        r = slice(256 * g, 256 * (g + 1))
        for d in range(8 * g, 8 * g + 8):
            if d > 0:
                back_s[d].wait_recv()
        return nn(ghi[:, r], ys[r, :]) + nn(glo[:, r], ys[r, :])

    for g in range(2):
        base = 256 * g
        r = slice(base, base + 256)
        for m in (2 * g, 2 * g + 1):
            for d in range(4 * m, 4 * m + 4):
                if d > 0:
                    to_s[d].wait_recv()
            block = x.at[k, pl.ds(TOK * m, TOK), pl.ds(lane_s, 2 * PAIR)]
            forwards[4 + m] = remote(block, block, f_s.at[4 + m], f_r.at[4 + m], sibling)
            forwards[4 + m].start()
        for m in (2 * g, 2 * g + 1):
            block = x.at[k, pl.ds(TOK * m, TOK), pl.ds(lane_p, PAIR)]
            remote(block, block, pf_s.at[m], pf_r.at[m], partner).wait_recv()
            forwards[8 + m] = remote(block, block, f_s.at[8 + m], f_r.at[8 + m], sibling)
            forwards[8 + m].start()
        gacc[...] = nt(x[k, r, :], weights[0, k])
        uacc[...] = nt(x[k, r, :], weights[1, k])
        for m in (2 * g, 2 * g + 1):
            for i, lane, width in ((0, lane_e, PAIR), (4, lane_s, 2 * PAIR), (8, lane_p, PAIR)):
                block = x.at[other, pl.ds(TOK * m, TOK), pl.ds(lane, width)]
                remote(block, block, f_s.at[i + m], f_r.at[i + m], sibling).wait_recv()
        gate = gacc[...] + nt(x[other, r, :], weights[0, other])
        up = uacc[...] + nt(x[other, r, :], weights[1, other])
        norm = x[k, r, pl.ds(lane_s + 128, 128)].astype(F32)
        norm = norm[:, 52:53] + norm[:, 53:54]
        gate, up = gate * norm, up * norm
        activated = (gate * jax.nn.sigmoid(1.702 * gate) * (up + 1.0)).astype(BF16)
        for i, lane in ((0, lane_o), (1, lane_s)):
            csend[i, r, :] = nn(activated, weights[2, other, :, pl.ds(lane, 2 * PAIR)]).astype(BF16)
            j = 2 * g + i
            pairs[j] = remote(
                csend.at[i, pl.ds(base, 256)], crecv.at[i, pl.ds(base, 256)], c_s.at[j], c_r.at[j], sibling
            )
            pairs[j].start()
        owne[r, :] = nn(activated, weights[2, k, :, pl.ds(lane_o, 2 * PAIR)])
        pairs[2 * g].wait_recv()
        for m in (2 * g, 2 * g + 1):
            rm = slice(TOK * m, TOK * (m + 1))
            owne[rm, :] = owne[rm, :] + crecv[0, rm, :].astype(F32)
            psend[rm, :] = owne[rm, pl.ds(pl.multiple_of(PAIR * (1 - b), 128), PAIR)].astype(BF16)
            piece = pl.ds(TOK * m, TOK)
            swaps[m] = remote(psend.at[piece], precv.at[piece], p_s.at[m], p_r.at[m], partner)
            swaps[m].start()
        owns[...] = nn(activated, weights[2, k, :, pl.ds(lane_s, 2 * PAIR)])
        pairs[2 * g + 1].wait_recv()
        for d in range(8 * g, 8 * g + 8):
            blk = slice(CAP * d, CAP * (d + 1))
            block = (owns[CAP * d - base : CAP * (d + 1) - base, :] + crecv[1, blk, :].astype(F32)).astype(BF16)
            if d == 0:
                ys[blk, :] = block
            else:
                yssend[blk, :] = block
                piece = pl.ds(CAP * d, CAP)
                back_s[d] = remote(yssend.at[piece], ys.at[piece], ys_s.at[d], ys_r.at[d], {"seq": behind[d]})
                back_s[d].start()
        if g == 0:
            make_gates()
        else:
            finish_group(0)
    maccs[...] = sum_shared(0)
    finish_group(1)

    unit = jnp.where(
        lax.broadcasted_iota(jnp.int32, (PAIR, PAIR), 0) == lax.broadcasted_iota(jnp.int32, (PAIR, PAIR), 1),
        jnp.float32(1.0), jnp.float32(0.0),
    ).astype(BF16)
    maccs[...] = maccs[...] + sum_shared(1)
    finals = []
    for q in range(2):
        turned = nt(unit, maccs[:, PAIR * q : PAIR * (q + 1)].astype(BF16))
        msends[2 * q : 2 * q + 2] = turned.astype(BF16).reshape(2, PAD, TOK)
        for j in (2 * q, 2 * q + 1):
            device = {"exp": 2 * (far_half + j) + k}
            finals.append(remote(msends.at[j], mrecv.at[2 + lax.rem(z, 4)], m_s.at[2 + j], m_r.at[2 + lax.rem(z, 4)], device))
            finals[j].start()
    for d in range(1, 16):
        back_e[d].wait_recv()
    macce[...] = nn(ghi[...], ye[...]) + nn(glo[...], ye[...])
    turned = nt(unit, macce[...].astype(BF16))
    msende[...] = turned.astype(BF16).reshape(2, PAD, TOK)
    to_mate = remote(msende.at[1 - b], mrecv.at[0], m_s.at[0], m_r.at[0], partner)
    to_pair = [
        remote(msende.at[j], mrecv.at[1], m_s.at[j], m_r.at[1], {"exp": 2 * (2 * group + j) + k}) for j in range(2)
    ]

    @pl.when(b == mid)
    def _():
        to_mate.start()
        mrecv[0] = msende[b]

    @pl.when(b != mid)
    def _():
        to_pair[0].start()
        to_pair[1].start()

    total = hid[...]
    for j in range(4):
        remote(msends.at[j], mrecv.at[2 + j], m_s.at[2 + j], m_r.at[2 + j], partner).wait_recv()
        total = total + mrecv[2 + j].astype(F32)
    remote(msende.at[0], mrecv.at[1], m_s.at[0], m_r.at[1], partner).wait_recv()

    @pl.when(b != mid)
    def _():
        to_mate.wait_recv()

    total = total + mrecv[1].astype(F32) + mrecv[0].astype(F32)
    out_ref[...] = total[0:SHARE, :].astype(BF16)

    @pl.when(b == mid)
    def _():
        to_mate.wait_send()

    @pl.when(b != mid)
    def _():
        to_pair[0].wait_send()
        to_pair[1].wait_send()

    halo.wait_send()
    for copy in first + second[1:] + squares[1:] + gather + logit_copies + to_e[1:] + to_s[1:]:
        copy.wait_send()
    for copy in passed + forwards + pairs + swaps + back_s[1:] + back_e[1:] + finals:
        copy.wait_send()


def vmem(*shape, dtype=BF16):
    return pltpu.VMEM(shape, dtype)


def body(
    queries, keyvals, sinks, out_proj, residual, norm_gain, router_weight, route_ids, expert_in, expert_out
):
    z = lax.axis_index("exp") // 2
    kv = lax.dynamic_slice(keyvals, (0, 0, 64 * z), (TOK, 2, 64)).reshape(TOK, TOK)
    local = pl.BlockSpec(memory_space=pltpu.VMEM)
    far = pl.BlockSpec(memory_space=pltpu.HBM)
    sems = lambda n: pltpu.SemaphoreType.DMA((n,))
    mixed = pl.pallas_call(
        kernel,
        out_shape=jax.ShapeDtypeStruct((SHARE, TOK), BF16),
        in_specs=[local, local, local, far, local, local, local, local, far, far],
        out_specs=local,
        scratch_shapes=[
            vmem(D, 256),
            vmem(3, UNITS, D),
            vmem(2 * TOK, TOK),
            vmem(TOK, 256),
            vmem(32, TOK, dtype=F32),
            vmem(ROWS, TOK),
            vmem(D + 16, TOK, dtype=F32),
            vmem(8, PAD, TOK),
            vmem(8, PAD, TOK),
            vmem(8, PAD, TOK),
            vmem(8, PAD, TOK),
            vmem(PAD, TOK, dtype=F32),
            vmem(PAD, TOK, dtype=F32),
            vmem(2 * PAIR, PAIR, dtype=jnp.int32),
            vmem(2 * PAIR, PAIR),
            vmem(3, 2, PAIR, HALF),
            vmem(1, TOK, dtype=F32),
            vmem(16, 1, TOK, dtype=F32),
            vmem(32, TOK, dtype=F32),
            vmem(32, TOK, dtype=F32),
            vmem(32, TOK, dtype=F32),
            vmem(8, 32, TOK, dtype=F32),
            vmem(8, PAD, TOK),
            vmem(ROWS, PAIR),
            vmem(ROWS, 2 * PAIR),
            vmem(2, ROWS, HALF),
            vmem(32, TOK, dtype=F32),
            vmem(ROWS, TOK),
            vmem(ROWS, TOK),
            vmem(TOK, ROWS),
            vmem(TOK, ROWS),
            vmem(256, PAIR, dtype=F32),
            vmem(256, PAIR, dtype=F32),
            vmem(256, 2 * PAIR, dtype=F32),
            vmem(ROWS, 2 * PAIR, dtype=F32),
            vmem(2, ROWS, 2 * PAIR),
            vmem(2, ROWS, 2 * PAIR),
            vmem(ROWS, PAIR),
            vmem(ROWS, PAIR),
            vmem(ROWS, 2 * PAIR),
            vmem(ROWS, PAIR),
            vmem(ROWS, 2 * PAIR),
            vmem(ROWS, PAIR),
            vmem(TOK, 2 * PAIR, dtype=F32),
            vmem(TOK, PAIR, dtype=F32),
            vmem(4, PAD, TOK),
            vmem(2, PAD, TOK),
            vmem(6, PAD, TOK),
            *(sems(n) for n in (3, 2, 8, 8, 8, 8, 16, 16, 8, 8, 6, 7)),
            *(sems(n) for n in (16, 16, 16, 16, 4, 4, 12, 12, 4, 4, 4, 4, 16, 16, 16, 16, 6, 6)),
        ],
        compiler_params=pltpu.CompilerParams(
            collective_id=0, has_side_effects=True, vmem_limit_bytes=56 * 2**20
        ),
        name="layer",
    )(
        queries,
        kv,
        sinks.reshape(1, 4),
        out_proj.T,
        residual.T,
        norm_gain.reshape(1, SHARE),
        router_weight.T,
        route_ids.T,
        jnp.transpose(expert_in[0], (1, 2, 0)),
        expert_out[0],
    )
    return mixed.T


def solution(mesh):
    return jax.shard_map(
        body,
        mesh=mesh,
        in_specs=(
            P("seq", "exp"),
            P("seq", None, None),
            P("exp"),
            P("exp", None),
            P("seq", "exp"),
            P("exp"),
            P("exp", None),
            P("seq", None),
            P(("seq", "exp"), None, None, None),
            P(("seq", "exp"), None, None),
        ),
        out_specs=P("seq", "exp"),
        check_vma=False,
    )
```

time: 104 us -> 85.8 us (0.82)
  Pallas kernels: 99.4 us -> 82.2 us
    pallas_call x1, Pallas kernels: 99.4 us -> 82.2 us  [body(): pl.pallas_call(kernel, out_shape=jax.ShapeDtypeStruct((SHARE, TOK), BF16)...]
where the time goes in v2:
time: 85.8 us; the launch traced here: 85.6 us
  Pallas kernels  82.2 us (96%)
  local copies, waits for them, and re-layouts  3.33 us (4%)
    pallas_call x1, Pallas kernels, body(): pl.pallas_call(kernel, out_shape=jax.ShapeDtypeStruct((SHARE, TOK), BF16)...  82.2 us
    unnamed x4, local copies, waits for them, and re-layouts  2.46 us

profile of v2, /device:TPU:64, one launch (start us, length us, event | category | flops | bytes accessed | tf_op | source)
XLA Modules:
  0.0 85.6 jit_solution(8720112937621101413)
XLA Ops:
  0.0 0.0 copy-start
  0.0 0.9 %copy-done = bf16[128,2,512]{2,1,0:T(2,128)(2,1)S(1)} copy-done((bf16[128,2,512]{2,1,0:T(2,128)(2,1)S(1)}, bf16[128,2,512]{2,1,0:T(2,128)(2,1)}, u32[]{:S(2)}) %copy-start) | copy-done | bytes 262168
  1.0 0.1 constant_dynamic-slice_fusion
  1.1 0.1 copy.13
  1.2 0.7 copy.12.kv_ref
  1.9 82.2 %layer.1 = bf16[180,128]{1,0:T(8,128)(2,1)} custom-call(bf16[128,256]{1,0:T(8,128)(2,1)} %q_ref.1, bf16[128,128]{1,0:T(8,128)(2,1)} %copy.12.kv_ref, f32[1,4]{1,0:T(1,128)} %bitcast.21, bf16[2880,256]{1,0:T(8,128)(2,1)} %bitcast.14, bf16[180,128]{1,0:T(8,128)(2,1)} %bitcast.17, f32[1,180]{1,0:T(1,128)} %bitcast.20, f32[32,180]{1,0:T(8,128)} %bitcast.18, ...), custom_call_target="tpu_custom_call" | custom-call | tf_op jit(solution)/shard_map/layer/pallas_call | solution.py:486
  84.2 1.4 %copy.15 = bf16[128,180]{0,1:T(8,128)(2,1)} copy(bf16[128,180]{0,1:T(8,128)(2,1)} %bitcast.15) | data formatting | bytes 92160
Async XLA Ops:
  0.0 1.0 %copy-start = (bf16[128,2,512]{2,1,0:T(2,128)(2,1)S(1)}, bf16[128,2,512]{2,1,0:T(2,128)(2,1)}, u32[]{:S(2)}) copy-start(bf16[128,2,512]{2,1,0:T(2,128)(2,1)} %param.11) | copy-start | bytes 786436

commit v3 on v2

--- a/solution.py
+++ b/solution.py
@@ -33,8 +33,9 @@
 
 
 def kernel(
-    q_ref, kv_ref, sink_ref, proj_hbm, res_ref, gain_ref, router_ref, route_ref, win_hbm, wout_hbm,
+    q_hbm, kv_hbm, sink_hbm, proj_hbm, res_hbm, gain_hbm, router_hbm, route_hbm, win_hbm, wout_hbm,
     out_ref,
+    q_ref, sink_ref, res_ref, gain_ref, router_ref, route_ref,
     proj, stage, kvall, wide, codes, pick, part, sibsend, sibrecv, rsend, rrecv, hid, mine,
     diff, sel, weights, sqsend, sqrecv, lgsend, lgsib, lgsum, lgrecv, xg, esend, ssend, x, gates, gthi, gtlo, ghi, glo,
     gacc, uacc, owns, owne, csend, crecv, psend, precv, yssend, yesend, ys, ye, maccs, macce, msends, msende, mrecv,
@@ -68,14 +69,23 @@
     for d in range(1, 16):
         pl.semaphore_signal(barrier, inc=1, device_id={"seq": ahead[d]}, device_id_type=MESH)
         pl.semaphore_signal(barrier, inc=1, device_id={"exp": lax.rem(e + d, 16)}, device_id_type=MESH)
+    small = [
+        pltpu.make_async_copy(source, target, load_sem.at[3 + i])
+        for i, (source, target) in enumerate((
+            (route_hbm, route_ref), (kv_hbm, kvall.at[pl.ds(TOK, TOK)]), (q_hbm, q_ref), (sink_hbm, sink_ref),
+            (res_hbm, res_ref), (gain_hbm, gain_ref), (router_hbm, router_ref),
+        ))
+    ]
+    for copy in small:
+        copy.start()
     load_proj = pltpu.make_async_copy(proj_hbm, proj, load_sem.at[0])
     load_in = pltpu.make_async_copy(win_hbm, stage.at[pl.ds(0, 2)], load_sem.at[1])
     load_out = pltpu.make_async_copy(wout_hbm, stage.at[2], load_sem.at[2])
     load_proj.start()
     load_in.start()
     load_out.start()
-    kvall[TOK:, :] = kv_ref[...]
-
+
+    small[0].wait()
     expert = lax.broadcasted_iota(jnp.int32, (32, TOK), 0)
     named = route_ref[0:1, :] == expert
     for j in range(1, 4):
@@ -93,7 +103,7 @@
         pick[CAP * d : CAP * (d + 1), :] = jnp.where(code == row, jnp.float32(1.0), jnp.float32(0.0)).astype(BF16)
 
     pl.semaphore_wait(barrier, 30)
-    halo = remote(kv_ref, kvall.at[pl.ds(0, TOK)], halo_sem.at[0], halo_sem.at[1], {"seq": lax.rem(s + 1, 16)})
+    halo = remote(kv_hbm, kvall.at[pl.ds(0, TOK)], halo_sem.at[0], halo_sem.at[1], {"seq": lax.rem(s + 1, 16)})
     halo.start()
     weights[...] = jnp.zeros_like(weights)
 
@@ -109,6 +119,8 @@
 
     qpos = lax.broadcasted_iota(jnp.int32, (TOK, TOK), 0)
     kpos = lax.broadcasted_iota(jnp.int32, (TOK, TOK), 1)
+    for i in (1, 2, 3):
+        small[i].wait()
     keys, values = sides(kvall[TOK:, :])
     new = []
     for head in range(4):
@@ -146,20 +158,19 @@
     lax.fori_loop(0, 5, project, 0)
     part[D : D + 16, :] = jnp.zeros((16, TOK), F32)
     order = (4, 3, 5, 2, 6, 1, 7, 0)
-    first, second = [None] * 8, [None] * 8
-    for d in order:
-        sibsend[d] = part[pl.ds(SHARE * (2 * zup[d] + other), PAD), :].astype(BF16)
-        first[d] = remote(sibsend.at[d], sibrecv.at[d], sib_s.at[d], sib_r.at[d], sibling)
-        first[d].start()
-    for d in order:
-        first[d].wait_recv()
-        pair_sum = part[pl.ds(SHARE * (2 * zup[d] + k), PAD), :] + sibrecv[d].astype(F32)
+    for i, d in enumerate(order):
+        sibsend[i] = part[pl.ds(SHARE * (2 * zup[d] + other), PAD), :].astype(BF16)
+        remote(sibsend.at[i], sibrecv.at[i], sib_s.at[0], sib_r.at[i // 4], sibling).start()
+    for i, d in enumerate(order):
+        if i % 4 == 0:
+            block = pl.ds(i, 4)
+            remote(sibsend.at[block], sibrecv.at[block], sib_s.at[0], sib_r.at[i // 4], sibling).wait_recv()
+        pair_sum = part[pl.ds(SHARE * (2 * zup[d] + k), PAD), :] + sibrecv[i].astype(F32)
         if d == 0:
             mine[...] = pair_sum
         else:
             rsend[d] = pair_sum.astype(BF16)
-            second[d] = remote(rsend.at[d], rrecv.at[d], rs_s.at[d], rs_r.at[d], {"exp": 2 * zup[d] + k})
-            second[d].start()
+            remote(rsend.at[d], rrecv.at[d], rs_s.at[0], rs_r.at[0], {"exp": 2 * zup[d] + k}).start()
 
     load_in.wait()
     ji = lax.broadcasted_iota(jnp.int32, (2 * PAIR, PAIR), 1)
@@ -196,9 +207,13 @@
     spread(0, 2)
 
     total = mine[...]
-    for d in (1, 7, 2, 6, 3, 5, 4):
-        second[d].wait_recv()
+    seven = pl.ds(1, 7)
+    second = remote(rsend.at[seven], rrecv.at[seven], rs_s.at[0], rs_r.at[0], partner)
+    second.wait_recv()
+    for d in range(1, 8):
         total = total + rrecv[d].astype(F32)
+    for i in (4, 5, 6):
+        small[i].wait()
     hid[SHARE - 4 :, :] = jnp.zeros((PAD - SHARE + 4, TOK), F32)
     hid[0:SHARE, :] = res_ref[...].astype(F32) + total[0:SHARE, :]
     state = hid[...]
@@ -207,38 +222,30 @@
     scaled = state * gain
     xg[z] = scaled.astype(BF16)
     sqsend[...] = jnp.sum(state * state, axis=0, keepdims=True)
-    gather = [
-        remote(xg.at[z], xg.at[z], ag_s.at[0], ag_r.at[0], partner),
-        remote(xg.at[z], xg.at[z], ag_s.at[1], ag_r.at[1 + b], {"exp": 2 * (4 * h + 2 - mid) + k}),
-    ]
-    for j in range(4):
-        device = {"exp": 2 * (far_half + j) + k}
-        gather.append(remote(xg.at[z], xg.at[z], ag_s.at[2 + j], ag_r.at[3 + lax.rem(z, 4)], device))
-    gather[0].start()
-    gather[1].start()
-    squares = [None] * 16
+    def gather(device, recv):
+        remote(xg.at[z], xg.at[z], ag_s.at[0], ag_r.at[recv], device).start()
+
+    gather(partner, 0)
+    gather({"exp": 2 * (4 * h + 2 - mid) + k}, 1)
     for d in range(1, 16):
         device = {"exp": lax.rem(e + d, 16)}
-        squares[d] = remote(sqsend, sqrecv.at[d], sq_s.at[d], sq_r.at[d], device)
-        squares[d].start()
-    for j in range(4):
-        gather[2 + j].start()
+        remote(sqsend, sqrecv.at[d], sq_s.at[0], sq_r.at[0], device).start()
+    for i in range(2):
+        gather({"exp": 2 * (far_half + 2 * i + b) + k}, 2 + mid)
     lgsend[...] = jnp.dot(
         router_ref[...], scaled[0:SHARE, :], precision=lax.Precision.HIGHEST, preferred_element_type=F32
     )
-    logit_copies = [remote(lgsend, lgsib, lg_s.at[0], lg_r.at[0], sibling)]
-    logit_copies[0].start()
-    def arrived(slot, sem):
-        remote(xg.at[slot], xg.at[slot], ag_s.at[0], ag_r.at[sem], partner).wait_recv()
-
-    arrived(mate, 0)
+    lg_first = remote(lgsend, lgsib, lg_s.at[0], lg_r.at[0], sibling)
+    lg_first.start()
+    def arrived(slots, sem):
+        remote(xg.at[slots], xg.at[slots], ag_s.at[0], ag_r.at[sem], partner).wait_recv()
+
+    arrived(pl.ds(mate, 1), 0)
 
     @pl.when(b != mid)
     def _():
-        arrived(4 * h + 2 * (1 - mid), 1)
-        arrived(4 * h + 2 * (1 - mid) + 1, 2)
-
-    to_e, to_s = [None] * 16, [None] * 16
+        arrived(pl.ds(4 * h + 2 * (1 - mid), 2), 1)
+
     features = xg[pl.ds(2 * group, 2)].reshape(PAIR, TOK)
     for g in range(4):
         r = slice(TOK * g, TOK * (g + 1))
@@ -250,35 +257,49 @@
             else:
                 piece = pl.ds(CAP * d, CAP)
                 target = x.at[k, piece, pl.ds(lane_e, PAIR)]
-                to_e[d] = remote(esend.at[piece], target, de_s.at[d], de_r.at[d], {"seq": ahead[d]})
-                to_e[d].start()
-
-    passed, forwards = [None] * 4, [None] * 12
+                remote(esend.at[piece], target, de_s.at[0], de_r.at[g], {"seq": ahead[d]}).start()
+
+    def came(g, lane, width, recv):
+        piece = pl.ds(CAP, TOK - CAP) if g == 0 else pl.ds(TOK * g, TOK)
+        block = x.at[k, piece, pl.ds(lane, width)]
+        remote(block, block, de_s.at[0], recv.at[g], partner).wait_recv()
+
+    def forward(g, lane, width):
+        block = x.at[k, pl.ds(TOK * g, TOK), pl.ds(lane, width)]
+        remote(block, block, f_s.at[0], f_r.at[g // 2], sibling).start()
 
     def pass_on(g):
-        for d in range(4 * g, 4 * g + 4):
-            if d > 0:
-                to_e[d].wait_recv()
+        came(g, lane_e, PAIR, de_r)
         block = x.at[k, pl.ds(TOK * g, TOK), pl.ds(lane_e, PAIR)]
-        passed[g] = remote(block, block, pf_s.at[g], pf_r.at[g], partner)
-        passed[g].start()
-        forwards[g] = remote(block, block, f_s.at[g], f_r.at[g], sibling)
-        forwards[g].start()
-
+        remote(block, block, pf_s.at[0], pf_r.at[g], partner).start()
+        forward(g, lane_e, PAIR)
+
+    for i in range(2):
+        slot = far_half + 2 * i + b
+        arrived(pl.ds(slot, 1), 2 + i)
+        remote(xg.at[slot], xg.at[slot], ag_s.at[0], ag_r.at[4 + i], partner).start()
     pass_on(0)
     pass_on(1)
-    for j in range(4):
-        arrived(far_half + j, 3 + j)
+    lg_first.wait_recv()
+    lgsum[...] = lgsend[...] + lgsib[...]
+    for d in range(1, 8):
+        remote(lgsum, lgrecv.at[d], lg_s.at[1], lg_r.at[1], {"exp": 2 * zup[d] + k}).start()
+    lg_second = remote(lgrecv.at[seven], lgrecv.at[seven], lg_s.at[1], lg_r.at[1], partner)
+    for i in range(2):
+        arrived(pl.ds(far_half + 2 * i + 1 - b, 1), 4 + i)
     square = sqsend[...]
+    fifteen = pl.ds(1, 15)
+    squares = remote(sqrecv.at[fifteen], sqrecv.at[fifteen], sq_s.at[0], sq_r.at[0], partner)
+    squares.wait_recv()
     for d in range(1, 16):
-        squares[d].wait_recv()
         square = square + sqrecv[d]
     factor = lax.rsqrt(square / D + EPS)
     high = factor.astype(BF16).astype(F32)
     ti = lax.broadcasted_iota(jnp.int32, (16, TOK), 0)
-    tail = xg[far_half, PAD - 16 :, :].astype(F32)
+    spare = far_half + 1 - b
+    tail = xg[spare, PAD - 16 :, :].astype(F32)
     tail = jnp.where(ti == 4, high, jnp.where(ti == 5, factor - high, tail))
-    xg[far_half, PAD - 16 :, :] = tail.astype(BF16)
+    xg[spare, PAD - 16 :, :] = tail.astype(BF16)
     for g in range(4):
         r = slice(TOK * g, TOK * (g + 1))
         for q in range(2):
@@ -290,17 +311,10 @@
             else:
                 piece = pl.ds(CAP * d, CAP)
                 target = x.at[k, piece, pl.ds(lane_s, 2 * PAIR)]
-                to_s[d] = remote(ssend.at[piece], target, ds_s.at[d], ds_r.at[d], {"seq": ahead[d]})
-                to_s[d].start()
+                remote(ssend.at[piece], target, ds_s.at[0], ds_r.at[g], {"seq": ahead[d]}).start()
     pass_on(2)
     pass_on(3)
 
-    logit_copies[0].wait_recv()
-    lgsum[...] = lgsend[...] + lgsib[...]
-    for d in range(1, 8):
-        device = {"exp": 2 * zup[d] + k}
-        logit_copies.append(remote(lgsum, lgrecv.at[d], lg_s.at[d], lg_r.at[d], device))
-        logit_copies[d].start()
     unit = jnp.where(
         lax.broadcasted_iota(jnp.int32, (TOK, TOK), 0) == lax.broadcasted_iota(jnp.int32, (TOK, TOK), 1),
         jnp.float32(1.0), jnp.float32(0.0),
@@ -311,8 +325,8 @@
 
     def make_gates():
         logits = lgsum[...]
+        lg_second.wait_recv()
         for d in range(1, 8):
-            logit_copies[d].wait_recv()
             logits = logits + lgrecv[d]
         raised = jnp.where(named > 0.0, jnp.exp(logits * factor), jnp.float32(0.0))
         gates[...] = raised / jnp.sum(raised, axis=0, keepdims=True)
@@ -324,7 +338,7 @@
         ghi[...] = nt(unit, gthi[...]).astype(BF16)
         glo[...] = nt(unit, gtlo[...]).astype(BF16)
 
-    back_s, back_e, pairs, swaps = [None] * 16, [None] * 16, [None] * 4, [None] * 4
+    swaps = [None] * 4
 
     def finish_group(g):
         for d in range(8 * g, 8 * g + 8):
@@ -337,71 +351,67 @@
             else:
                 yesend[blk, :] = block.astype(BF16)
                 piece = pl.ds(CAP * d, CAP)
-                back_e[d] = remote(yesend.at[piece], ye.at[piece], ye_s.at[d], ye_r.at[d], {"seq": behind[d]})
-                back_e[d].start()
+                remote(yesend.at[piece], ye.at[piece], ye_s.at[0], ye_r.at[0], {"seq": behind[d]}).start()
 
     def sum_shared(g):
         r = slice(256 * g, 256 * (g + 1))
-        for d in range(8 * g, 8 * g + 8):
-            if d > 0:
-                back_s[d].wait_recv()
+        piece = pl.ds(CAP, 256 - CAP) if g == 0 else pl.ds(256, 256)
+        remote(yssend.at[piece], ys.at[piece], ys_s.at[0], ys_r.at[g], partner).wait_recv()
         return nn(ghi[:, r], ys[r, :]) + nn(glo[:, r], ys[r, :])
 
     for g in range(2):
         base = 256 * g
         r = slice(base, base + 256)
         for m in (2 * g, 2 * g + 1):
-            for d in range(4 * m, 4 * m + 4):
-                if d > 0:
-                    to_s[d].wait_recv()
-            block = x.at[k, pl.ds(TOK * m, TOK), pl.ds(lane_s, 2 * PAIR)]
-            forwards[4 + m] = remote(block, block, f_s.at[4 + m], f_r.at[4 + m], sibling)
-            forwards[4 + m].start()
+            came(m, lane_s, 2 * PAIR, ds_r)
+            forward(m, lane_s, 2 * PAIR)
         for m in (2 * g, 2 * g + 1):
             block = x.at[k, pl.ds(TOK * m, TOK), pl.ds(lane_p, PAIR)]
-            remote(block, block, pf_s.at[m], pf_r.at[m], partner).wait_recv()
-            forwards[8 + m] = remote(block, block, f_s.at[8 + m], f_r.at[8 + m], sibling)
-            forwards[8 + m].start()
+            remote(block, block, pf_s.at[0], pf_r.at[m], partner).wait_recv()
+            forward(m, lane_p, PAIR)
         gacc[...] = nt(x[k, r, :], weights[0, k])
         uacc[...] = nt(x[k, r, :], weights[1, k])
-        for m in (2 * g, 2 * g + 1):
-            for i, lane, width in ((0, lane_e, PAIR), (4, lane_s, 2 * PAIR), (8, lane_p, PAIR)):
-                block = x.at[other, pl.ds(TOK * m, TOK), pl.ds(lane, width)]
-                remote(block, block, f_s.at[i + m], f_r.at[i + m], sibling).wait_recv()
+        block = x.at[other, pl.ds(base, 256)]
+        remote(block, block, f_s.at[0], f_r.at[g], sibling).wait_recv()
         gate = gacc[...] + nt(x[other, r, :], weights[0, other])
         up = uacc[...] + nt(x[other, r, :], weights[1, other])
-        norm = x[k, r, pl.ds(lane_s + 128, 128)].astype(F32)
-        norm = norm[:, 52:53] + norm[:, 53:54]
+        norm = x[k, r, pl.ds(pl.multiple_of(lane_s + 128 * (2 - b), 128), 128)].astype(F32)
+        lane = lax.broadcasted_iota(jnp.int32, (256, 128), 1) - jnp.where(b == 0, 116, 52)
+        norm = jnp.sum(jnp.where((lane == 0) | (lane == 1), norm, jnp.float32(0.0)), axis=1, keepdims=True)
         gate, up = gate * norm, up * norm
         activated = (gate * jax.nn.sigmoid(1.702 * gate) * (up + 1.0)).astype(BF16)
-        for i, lane in ((0, lane_o), (1, lane_s)):
-            csend[i, r, :] = nn(activated, weights[2, other, :, pl.ds(lane, 2 * PAIR)]).astype(BF16)
-            j = 2 * g + i
-            pairs[j] = remote(
-                csend.at[i, pl.ds(base, 256)], crecv.at[i, pl.ds(base, 256)], c_s.at[j], c_r.at[j], sibling
-            )
-            pairs[j].start()
-        owne[r, :] = nn(activated, weights[2, k, :, pl.ds(lane_o, 2 * PAIR)])
-        pairs[2 * g].wait_recv()
-        for m in (2 * g, 2 * g + 1):
-            rm = slice(TOK * m, TOK * (m + 1))
-            owne[rm, :] = owne[rm, :] + crecv[0, rm, :].astype(F32)
-            psend[rm, :] = owne[rm, pl.ds(pl.multiple_of(PAIR * (1 - b), 128), PAIR)].astype(BF16)
-            piece = pl.ds(TOK * m, TOK)
-            swaps[m] = remote(psend.at[piece], precv.at[piece], p_s.at[m], p_r.at[m], partner)
-            swaps[m].start()
-        owns[...] = nn(activated, weights[2, k, :, pl.ds(lane_s, 2 * PAIR)])
-        pairs[2 * g + 1].wait_recv()
-        for d in range(8 * g, 8 * g + 8):
-            blk = slice(CAP * d, CAP * (d + 1))
-            block = (owns[CAP * d - base : CAP * (d + 1) - base, :] + crecv[1, blk, :].astype(F32)).astype(BF16)
-            if d == 0:
-                ys[blk, :] = block
-            else:
-                yssend[blk, :] = block
-                piece = pl.ds(CAP * d, CAP)
-                back_s[d] = remote(yssend.at[piece], ys.at[piece], ys_s.at[d], ys_r.at[d], {"seq": behind[d]})
-                back_s[d].start()
+        pairs = [None] * 2
+        lanes = (lane_o, lane_s)
+        sequence = (1, 0) if g == 0 else (0, 1)
+        for i in sequence:
+            csend[i, r, :] = nn(activated, weights[2, other, :, pl.ds(lanes[i], 2 * PAIR)]).astype(BF16)
+            piece = pl.ds(base, 256)
+            pairs[i] = remote(csend.at[i, piece], crecv.at[i, piece], c_s.at[0], c_r.at[2 * g + i], sibling)
+            pairs[i].start()
+        for i in sequence:
+            product = nn(activated, weights[2, k, :, pl.ds(lanes[i], 2 * PAIR)])
+            if i == 0:
+                owne[r, :] = product
+                pairs[0].wait_recv()
+                for m in (2 * g, 2 * g + 1):
+                    rm = slice(TOK * m, TOK * (m + 1))
+                    owne[rm, :] = owne[rm, :] + crecv[0, rm, :].astype(F32)
+                    psend[rm, :] = owne[rm, pl.ds(pl.multiple_of(PAIR * (1 - b), 128), PAIR)].astype(BF16)
+                    piece = pl.ds(TOK * m, TOK)
+                    swaps[m] = remote(psend.at[piece], precv.at[piece], p_s.at[0], p_r.at[m], partner)
+                    swaps[m].start()
+                continue
+            owns[...] = product
+            pairs[1].wait_recv()
+            for d in range(8 * g, 8 * g + 8):
+                blk = slice(CAP * d, CAP * (d + 1))
+                block = owns[CAP * d - base : CAP * (d + 1) - base, :] + crecv[1, blk, :].astype(F32)
+                if d == 0:
+                    ys[blk, :] = block.astype(BF16)
+                else:
+                    yssend[blk, :] = block.astype(BF16)
+                    piece = pl.ds(CAP * d, CAP)
+                    remote(yssend.at[piece], ys.at[piece], ys_s.at[0], ys_r.at[g], {"seq": behind[d]}).start()
         if g == 0:
             make_gates()
         else:
@@ -414,23 +424,19 @@
         jnp.float32(1.0), jnp.float32(0.0),
     ).astype(BF16)
     maccs[...] = maccs[...] + sum_shared(1)
-    finals = []
     for q in range(2):
         turned = nt(unit, maccs[:, PAIR * q : PAIR * (q + 1)].astype(BF16))
         msends[2 * q : 2 * q + 2] = turned.astype(BF16).reshape(2, PAD, TOK)
         for j in (2 * q, 2 * q + 1):
             device = {"exp": 2 * (far_half + j) + k}
-            finals.append(remote(msends.at[j], mrecv.at[2 + lax.rem(z, 4)], m_s.at[2 + j], m_r.at[2 + lax.rem(z, 4)], device))
-            finals[j].start()
-    for d in range(1, 16):
-        back_e[d].wait_recv()
+            remote(msends.at[j], mrecv.at[2 + lax.rem(z, 4)], m_s.at[0], m_r.at[2], device).start()
+    others = pl.ds(CAP, ROWS - CAP)
+    back_e = remote(yesend.at[others], ye.at[others], ye_s.at[0], ye_r.at[0], partner)
+    back_e.wait_recv()
     macce[...] = nn(ghi[...], ye[...]) + nn(glo[...], ye[...])
     turned = nt(unit, macce[...].astype(BF16))
     msende[...] = turned.astype(BF16).reshape(2, PAD, TOK)
-    to_mate = remote(msende.at[1 - b], mrecv.at[0], m_s.at[0], m_r.at[0], partner)
-    to_pair = [
-        remote(msende.at[j], mrecv.at[1], m_s.at[j], m_r.at[1], {"exp": 2 * (2 * group + j) + k}) for j in range(2)
-    ]
+    to_mate = remote(msende.at[1 - b], mrecv.at[0], m_s.at[1], m_r.at[0], partner)
 
     @pl.when(b == mid)
     def _():
@@ -439,14 +445,15 @@
 
     @pl.when(b != mid)
     def _():
-        to_pair[0].start()
-        to_pair[1].start()
-
+        for j in range(2):
+            remote(msende.at[j], mrecv.at[1], m_s.at[1], m_r.at[1], {"exp": 2 * (2 * group + j) + k}).start()
+
+    far_four = remote(msends, mrecv.at[pl.ds(2, 4)], m_s.at[0], m_r.at[2], partner)
+    far_four.wait_recv()
     total = hid[...]
     for j in range(4):
-        remote(msends.at[j], mrecv.at[2 + j], m_s.at[2 + j], m_r.at[2 + j], partner).wait_recv()
         total = total + mrecv[2 + j].astype(F32)
-    remote(msende.at[0], mrecv.at[1], m_s.at[0], m_r.at[1], partner).wait_recv()
+    remote(msende.at[0], mrecv.at[1], m_s.at[1], m_r.at[1], partner).wait_recv()
 
     @pl.when(b != mid)
     def _():
@@ -461,13 +468,21 @@
 
     @pl.when(b != mid)
     def _():
-        to_pair[0].wait_send()
-        to_pair[1].wait_send()
-
-    halo.wait_send()
-    for copy in first + second[1:] + squares[1:] + gather + logit_copies + to_e[1:] + to_s[1:]:
-        copy.wait_send()
-    for copy in passed + forwards + pairs + swaps + back_s[1:] + back_e[1:] + finals:
+        remote(msende, msende, m_s.at[1], m_r.at[1], partner).wait_send()
+
+    def sent(ref, sem):
+        remote(ref, ref, sem, sem, partner).wait_send()
+
+    sent(sibsend, sib_s.at[0])
+    sent(xg.at[pl.ds(0, 6)], ag_s.at[0])
+    sent(esend.at[others], de_s.at[0])
+    sent(ssend.at[others], ds_s.at[0])
+    sent(esend, pf_s.at[0])
+    sent(x.at[k], f_s.at[0])
+    sent(csend, c_s.at[0])
+    sent(psend, p_s.at[0])
+    sent(yssend.at[others], ys_s.at[0])
+    for copy in (halo, second, squares, lg_first, lg_second, back_e, far_four):
         copy.wait_send()
 
 
@@ -486,9 +501,15 @@
     mixed = pl.pallas_call(
         kernel,
         out_shape=jax.ShapeDtypeStruct((SHARE, TOK), BF16),
-        in_specs=[local, local, local, far, local, local, local, local, far, far],
+        in_specs=[far] * 10,
         out_specs=local,
         scratch_shapes=[
+            vmem(TOK, 256),
+            vmem(1, 4, dtype=F32),
+            vmem(SHARE, TOK),
+            vmem(1, SHARE, dtype=F32),
+            vmem(32, SHARE, dtype=F32),
+            vmem(4, TOK, dtype=jnp.int32),
             vmem(D, 256),
             vmem(3, UNITS, D),
             vmem(2 * TOK, TOK),
@@ -537,8 +558,8 @@
             vmem(4, PAD, TOK),
             vmem(2, PAD, TOK),
             vmem(6, PAD, TOK),
-            *(sems(n) for n in (3, 2, 8, 8, 8, 8, 16, 16, 8, 8, 6, 7)),
-            *(sems(n) for n in (16, 16, 16, 16, 4, 4, 12, 12, 4, 4, 4, 4, 16, 16, 16, 16, 6, 6)),
+            *(sems(n) for n in (10, 2, 1, 2, 1, 1, 1, 1, 2, 2, 1, 6)),
+            *(sems(n) for n in (1, 4, 1, 4, 1, 4, 1, 2, 1, 4, 1, 4, 1, 2, 1, 1, 2, 3)),
         ],
         compiler_params=pltpu.CompilerParams(
             collective_id=0, has_side_effects=True, vmem_limit_bytes=56 * 2**20

time: 85.8 us -> 80.4 us (0.937)
  Pallas kernels: 82.2 us -> 76.2 us
    pallas_call x1, Pallas kernels: 82.2 us -> 76.2 us  [body(): pl.pallas_call(kernel, out_shape=jax.ShapeDtypeStruct((SHARE, TOK), BF16)...]
where the time goes in v3:
time: 80.4 us; the launch traced here: 79.5 us
  Pallas kernels  76.2 us (95%)
  local copies, waits for them, and re-layouts  3.33 us (4%)
    pallas_call x1, Pallas kernels, body(): pl.pallas_call(kernel, out_shape=jax.ShapeDtypeStruct((SHARE, TOK), BF16)...  76.2 us
    unnamed x4, local copies, waits for them, and re-layouts  2.46 us

profile of v3, /device:TPU:64, one launch (start us, length us, event | category | flops | bytes accessed | tf_op | source)
XLA Modules:
  0.0 79.5 jit_solution(17230879027484572131)
XLA Ops:
  0.0 0.0 copy-start
  0.0 0.9 %copy-done = bf16[128,2,512]{2,1,0:T(2,128)(2,1)S(1)} copy-done((bf16[128,2,512]{2,1,0:T(2,128)(2,1)S(1)}, bf16[128,2,512]{2,1,0:T(2,128)(2,1)}, u32[]{:S(2)}) %copy-start) | copy-done | bytes 262168
  1.0 0.1 constant_dynamic-slice_fusion
  1.1 0.1 copy.13
  1.2 0.7 copy.12.kv_hbm
  1.9 76.2 %layer.1 = bf16[180,128]{1,0:T(8,128)(2,1)} custom-call(bf16[128,256]{1,0:T(8,128)(2,1)} %q_hbm.1, bf16[128,128]{1,0:T(8,128)(2,1)} %copy.12.kv_hbm, f32[1,4]{1,0:T(1,128)} %bitcast.21, bf16[2880,256]{1,0:T(8,128)(2,1)} %bitcast.14, bf16[180,128]{1,0:T(8,128)(2,1)} %bitcast.17, f32[1,180]{1,0:T(1,128)} %bitcast.20, f32[32,180]{1,0:T(8,128)} %bitcast.18, ...), custom_call_target="tpu_custom_call" | custom-call | tf_op jit(solution)/shard_map/layer/pallas_call | solution.py:501
  78.1 1.4 %copy.15 = bf16[128,180]{0,1:T(8,128)(2,1)} copy(bf16[128,180]{0,1:T(8,128)(2,1)} %bitcast.15) | data formatting | bytes 92160
Async XLA Ops:
  0.0 1.0 %copy-start = (bf16[128,2,512]{2,1,0:T(2,128)(2,1)S(1)}, bf16[128,2,512]{2,1,0:T(2,128)(2,1)}, u32[]{:S(2)}) copy-start(bf16[128,2,512]{2,1,0:T(2,128)(2,1)} %param.11) | copy-start | bytes 786436

commit v4 on v3

--- a/solution.py
+++ b/solution.py
@@ -227,11 +227,11 @@
 
     gather(partner, 0)
     gather({"exp": 2 * (4 * h + 2 - mid) + k}, 1)
+    for i in range(2):
+        gather({"exp": 2 * (far_half + 2 * i + b) + k}, 2 + mid)
     for d in range(1, 16):
         device = {"exp": lax.rem(e + d, 16)}
         remote(sqsend, sqrecv.at[d], sq_s.at[0], sq_r.at[0], device).start()
-    for i in range(2):
-        gather({"exp": 2 * (far_half + 2 * i + b) + k}, 2 + mid)
     lgsend[...] = jnp.dot(
         router_ref[...], scaled[0:SHARE, :], precision=lax.Precision.HIGHEST, preferred_element_type=F32
     )
@@ -412,10 +412,9 @@
                     yssend[blk, :] = block.astype(BF16)
                     piece = pl.ds(CAP * d, CAP)
                     remote(yssend.at[piece], ys.at[piece], ys_s.at[0], ys_r.at[g], {"seq": behind[d]}).start()
-        if g == 0:
+        if g == 1:
+            finish_group(0)
             make_gates()
-        else:
-            finish_group(0)
     maccs[...] = sum_shared(0)
     finish_group(1)
 

time: 80.4 us -> 80.6 us (level)
  no operation moved by 1% of the time
where the time goes in v4:
time: 80.6 us; the launch traced here: 79.7 us
  Pallas kernels  76.4 us (95%)
  local copies, waits for them, and re-layouts  3.33 us (4%)
    pallas_call x1, Pallas kernels, body(): pl.pallas_call(kernel, out_shape=jax.ShapeDtypeStruct((SHARE, TOK), BF16)...  76.4 us
    unnamed x4, local copies, waits for them, and re-layouts  2.46 us

profile of v4, /device:TPU:64, one launch (start us, length us, event | category | flops | bytes accessed | tf_op | source)
XLA Modules:
  0.0 79.7 jit_solution(8140997174050768794)
XLA Ops:
  0.0 0.0 copy-start
  0.0 0.9 %copy-done = bf16[128,2,512]{2,1,0:T(2,128)(2,1)S(1)} copy-done((bf16[128,2,512]{2,1,0:T(2,128)(2,1)S(1)}, bf16[128,2,512]{2,1,0:T(2,128)(2,1)}, u32[]{:S(2)}) %copy-start) | copy-done | bytes 262168
  1.0 0.1 constant_dynamic-slice_fusion
  1.1 0.1 copy.13
  1.2 0.7 copy.12.kv_hbm
  1.9 76.4 %layer.1 = bf16[180,128]{1,0:T(8,128)(2,1)} custom-call(bf16[128,256]{1,0:T(8,128)(2,1)} %q_hbm.1, bf16[128,128]{1,0:T(8,128)(2,1)} %copy.12.kv_hbm, f32[1,4]{1,0:T(1,128)} %bitcast.21, bf16[2880,256]{1,0:T(8,128)(2,1)} %bitcast.14, bf16[180,128]{1,0:T(8,128)(2,1)} %bitcast.17, f32[1,180]{1,0:T(1,128)} %bitcast.20, f32[32,180]{1,0:T(8,128)} %bitcast.18, ...), custom_call_target="tpu_custom_call" | custom-call | tf_op jit(solution)/shard_map/layer/pallas_call | solution.py:500
  78.3 1.4 %copy.15 = bf16[128,180]{0,1:T(8,128)(2,1)} copy(bf16[128,180]{0,1:T(8,128)(2,1)} %bitcast.15) | data formatting | bytes 92160
Async XLA Ops:
  0.0 1.0 %copy-start = (bf16[128,2,512]{2,1,0:T(2,128)(2,1)S(1)}, bf16[128,2,512]{2,1,0:T(2,128)(2,1)}, u32[]{:S(2)}) copy-start(bf16[128,2,512]{2,1,0:T(2,128)(2,1)} %param.11) | copy-start | bytes 786436
